TPU v7x, 32 devices: a whole 2x2x4 slice. The times are simulated.
32 devices in a mesh: seq: 4 (over y, x), shard: 8 (over z, core).
Axes of the slice: x: 2, y: 2, z: 4, core: 2. Of those that a mesh axis runs over, the one named last changes fastest.
Arguments:
- tokens: bfloat16 [8192, 2048], P(('shard', 'seq')), may hold values from -6 to 6
- cotangent: bfloat16 [8192, 2048], P(('shard', 'seq')), may hold values from -6 to 6
- gain_attn: float32 [2048], replicated, may hold values from 0.5 to 1.5
- gain_ffn: float32 [2048], replicated, may hold values from 0.5 to 1.5
- mixer_in: bfloat16 [12288, 2048], P('shard'), may hold values from -0.088388348 to 0.088388348, as said below
- mixer_out: bfloat16 [2048, 4096], P('shard'), may hold values from -0.0625 to 0.0625, as said below
- ffn_in: bfloat16 [8192, 2048], P('shard'), may hold values from -0.088388348 to 0.088388348, as said below
- ffn_out: bfloat16 [2048, 4096], P('shard'), may hold values from -0.0625 to 0.0625, as said below
- segment_order: int32 [8], replicated, may hold values from 0 to 7, each once
- decay_index: int32 [8], replicated, may hold values from 0 to 11
Outputs:
- output: bfloat16 [8192, 2048], P(('shard', 'seq'))
- input_grad: bfloat16 [8192, 2048], P(('shard', 'seq'))
- gain_attn_grad: float32 [2048], replicated
- gain_ffn_grad: float32 [2048], replicated
- mixer_in_grad: float32 [12288, 2048], P('shard')
- mixer_out_grad: float32 [2048, 4096], P('shard')
- ffn_in_grad: float32 [8192, 2048], P('shard')
- ffn_out_grad: float32 [2048, 4096], P('shard')
Inputs may be any that keep to these rules, and one draw needn't show every extreme that they name: `segment_order`: a permutation: each place 0 to 7 once. `mixer_in`: independent entries of mean 0 and deviation 2048^-0.5. `mixer_out`: independent entries of mean 0 and deviation 4096^-0.5. `ffn_in`: independent entries of mean 0 and deviation 2048^-0.5. `ffn_out`: independent entries of mean 0 and deviation 4096^-0.5.
All inputs are finite; a program needn't handle non-finite values.
Results may differ from a plain program's by a relative error of at most 0.022.
Values may be sent and summed in bfloat16 or wider, within the bound.
No kernel may reach another device: no remote copies, remote signals or barrier semaphores. Data moves between devices by JAX's collectives and lax.ppermute only.
A program may use at most 512 MiB of HBM per device.

v0:
```python
import functools

import jax
import jax.numpy as jnp
import numpy as np
from jax import lax
from jax.experimental import pallas as pl
from jax.experimental.pallas import tpu as pltpu
from jax.sharding import PartitionSpec as P

DK = 256
DV = 512
FF = 4096
QK = 2048
V = 4096


EPS_NORM = 1e-06
EPS_GROUP = 1e-05

F32 = jnp.float32
BF16 = jnp.bfloat16


def dot_nt(left, right, kind=F32):
    return lax.dot_general(
        left, right, (((1,), (1,)), ((), ())), preferred_element_type=F32
    ).astype(kind)


def dot_nn(left, right, kind=F32):
    return lax.dot_general(
        left, right, (((1,), (0,)), ((), ())), preferred_element_type=F32
    ).astype(kind)


def dot_tn(left, right, kind=F32):
    return lax.dot_general(
        left, right, (((0,), (0,)), ((), ())), preferred_element_type=F32
    ).astype(kind)


def rms_scale(v, gain):
    return v * lax.rsqrt(jnp.mean(v * v, axis=-1, keepdims=True) + EPS_NORM) * gain


def gated_gelu(first, second):
    return jax.nn.gelu(first) * second


def unit_owners(heads):
    owners = [(n, 0) for n in range(heads)] + [(n, 1) for n in range(heads)]
    for base in (2, 4):
        owners += [(n, base + half) for n in range(heads) for half in range(2)]
    return owners


def balanced_tables():
    group, segments, per_shard = 4, 8, 6
    number = {owner: u for u, owner in enumerate(unit_owners(8))}
    keep = np.full((2, segments, group), -1, np.int32)
    give = np.zeros((2, segments, group), np.int32)
    back = np.zeros((segments, per_shard, 2), np.int32)
    lend = [[] for _ in range(segments)]
    seen = set()
    for s in range(group):
        a, b = s, s + 4
        if s < 2:
            gates = [(a, 4), (b, 4), (b, 5)], (b + 2, 5)
        else:
            gates = [(a - 2, 5), (a, 4), (a, 5)], (b, 4)
        first = [(a, 0), (a, 1), (a, 2), (a, 3), (b, 2)] + gates[0]
        second = [(b, 0), (b, 1), (b, 3), gates[1]]
        for slot, owner in enumerate(first):
            home, index = divmod(number[owner], per_shard)
            seen.add(number[owner])
            assert home // 2 == slot // 2
            if home == slot:
                keep[0, slot, s] = index
                back[home, index] = (0, s)
            else:
                give[0, home, s] = index
                back[home, index] = (1, len(lend[slot]))
                lend[slot].append(s)
        for chip, owner in enumerate(second):
            home, index = divmod(number[owner], per_shard)
            seen.add(number[owner])
            assert home // 2 == chip
            keep[1, home, s] = index
            give[1, home, s] = index
            back[home, index] = (2, s)
    assert len(seen) == segments * per_shard
    most = max(len(t) for t in lend)
    return keep, give, back, np.asarray([(t + [0] * most)[:most] for t in lend], np.int32)


def unit_tables(group, local_heads, segments):
    heads = group * local_heads
    owners = unit_owners(heads)
    per_shard = len(owners) // segments
    keep = np.full((local_heads, segments, group), -1, np.int32)
    give = np.zeros((local_heads, segments, group), np.int32)
    place = np.zeros((local_heads, group, 6), np.int32)
    held = np.full((local_heads, segments, group), -1, np.int32)
    slot_of = {}
    for chip in range(segments // 2):
        for head in range(heads):
            h, s = divmod(head, group)
            span = range(2 * per_shard * chip, 2 * per_shard * (chip + 1))
            mine = [u for u in span if owners[u][0] == head]
            assert len(mine) <= 2
            for n, u in enumerate(mine):
                home = u // per_shard
                slot = home if len(mine) == 1 else 2 * chip + n
                if slot == home:
                    keep[h, slot, s] = u % per_shard
                else:
                    give[h, home, s] = u % per_shard
                place[h, s, owners[u][1]] = slot
                held[h, slot, s] = owners[u][1]
                slot_of[u] = slot
    lends = [[[] for _ in range(segments)] for _ in range(local_heads)]
    back = np.zeros((segments, per_shard, 3), np.int32)
    for u, (head, _) in enumerate(owners):
        home = u // per_shard
        h, s = divmod(head, group)
        back[home, u % per_shard] = (h, s, -1)
        if slot_of[u] != home:
            assert slot_of[u] == home ^ 1
            back[home, u % per_shard, 2] = len(lends[h][home ^ 1])
            lends[h][home ^ 1].append(s)
    most = max(1, max(len(t) for row in lends for t in row))
    lend = np.asarray(
        [[(t + [0] * most)[:most] for t in row] for row in lends], np.int32
    )
    return keep, give, place, held, back, lend


def tie(*values):
    return lax.optimization_barrier(values)


def mm(left, right, dims):
    return lax.dot_general(left, right, (dims, ((), ())), preferred_element_type=F32)


NN = ((1,), (0,))
NT = ((1,), (1,))
TN = ((0,), (0,))


def turn(v, cosine, sine):
    half = v.shape[-1] // 2
    first, second = v[:, :half], v[:, half:]
    return jnp.concatenate(
        [first * cosine - second * sine, second * cosine + first * sine], axis=-1
    )


def scaled(v, decay):
    return (v.astype(F32) * decay).astype(BF16)


def project_kernel(blk, roles, carried, params, x, w, cosine, sine, k_decay, *refs):
    if carried:
        v_a, *refs = refs
    q, k, v, total, gates, *rest = refs
    y = rest[-1]
    rows = y.shape[0]
    y[...] = mm(x[...], w[...], NT)

    def put(role, part, gate_at):
        value = y[:, part * DK : (part + 1) * DK]
        if role == "q":
            q[...] = turn(value, cosine[...], sine[...]).astype(BF16)
        elif role == "k":
            k[...] = turn(value, cosine[...], sine[...]).astype(BF16)
        elif role == "va":
            v[:, :DK] = value.astype(BF16)
        elif role == "vb":
            v[:, DK:] = value.astype(BF16)
        elif role == "xv":
            rest[0][...] = value.astype(BF16)
        else:
            gates[:, gate_at * DK : (gate_at + 1) * DK] = value.astype(BF16)

    for step in range(len(roles) // 2):

        @pl.when(pl.program_id(0) == step)
        def _(step=step):
            for part in range(2):
                at = 2 * step + part
                put(roles[at], part, roles[:at].count("g"))
            if step == 1:
                if carried:
                    v[:, :DK] = v_a[...]
                state = jnp.zeros(total.shape, F32)
                for r in range(0, rows, blk):
                    kd = scaled(k[r : r + blk, :], k_decay[...])
                    state = params[0] * state + mm(kd, v[r : r + blk, :], TN)
                total[...] = state.astype(BF16)


def join_kernel(count, *refs):
    out = refs[-1]
    total = mm(refs[0][...], refs[count][...], NN)
    for n in range(1, count):
        total += mm(refs[n][...], refs[count + n][...], NN)
    out[...] = total.astype(out.dtype)


def select(params, low, high):
    return jnp.where(params[1] > 0.5, low[...].astype(F32), high[...].astype(F32))


def retain_kernel(
    params, q, k, v, low_a, high_a, low_b, high_b, mask, q_decay, k_decay, start,
    hidden, mixed, kept, state,
):
    @pl.when(pl.program_id(0) == 0)
    def _():
        state[...] = start[...].astype(F32)

    weights = (mm(q[...], k[...], NT) * mask[...]).astype(BF16)
    o = mm(weights, v[...], NN)
    o += mm(scaled(q[...], q_decay[...]), state[...].astype(BF16), NN)
    state[...] = params[0] * state[...] + mm(scaled(k[...], k_decay[...]), v[...], TN)
    o = o - jnp.mean(o, axis=-1, keepdims=True)
    inverse = lax.rsqrt(jnp.mean(o * o, axis=-1, keepdims=True) + EPS_GROUP)
    kept[...] = inverse
    low = (o * inverse).astype(BF16)
    mixed[...] = low
    for n, (one, two) in enumerate(((low_a, high_a), (low_b, high_b))):
        columns = slice(n * DK, (n + 1) * DK)
        g = select(params, one, two)
        hidden[:, columns] = (g * jax.nn.sigmoid(g) * low[:, columns].astype(F32)).astype(BF16)


def take(refs, counts):
    pieces, at = [], 0
    for count in counts:
        pieces.append(refs[at : at + count])
        at += count
    return pieces


def gate_back_kernel(heads, params, d_attn, w_out, *refs):
    inputs = take(refs, [8] * heads)
    outputs = take(refs[8 * heads :], [3] * heads)
    states = refs[11 * heads :]

    @pl.when(pl.program_id(0) == 0)
    def _():
        for state in states:
            state[...] = jnp.zeros(state.shape, F32)

    d_hidden = mm(d_attn[...], w_out[...], NN)
    for h in range(heads):
        low_a, high_a, low_b, high_b, mixed, inverse, q, q_decay = inputs[h]
        d_gate, d_out, total = outputs[h]
        g = jnp.concatenate(
            [select(params, low_a, high_a), select(params, low_b, high_b)], axis=1
        )
        dh = d_hidden[:, h * DV : (h + 1) * DV]
        sig = jax.nn.sigmoid(g)
        o = mixed[...].astype(F32)
        d_gate[...] = (dh * o * (sig * (1.0 + g * (1.0 - sig)))).astype(BF16)
        dy = (dh * (g * sig)).astype(BF16).astype(F32)
        do = inverse[...] * (
            dy
            - jnp.mean(dy, axis=-1, keepdims=True)
            - o * jnp.mean(dy * o, axis=-1, keepdims=True)
        )
        do = do.astype(BF16)
        d_out[...] = do
        state = states[h]
        state[...] = params[2 + h] * state[...] + mm(scaled(q[...], q_decay[...]), do, TN)
        total[...] = state[...].astype(BF16)


def inner_back_kernel(heads, params, cosine, sine, *refs):
    inputs = take(refs, [8] * heads)
    outputs = take(refs[8 * heads :], [3] * heads)
    states = refs[11 * heads :]

    @pl.when(pl.program_id(0) == 0)
    def _():
        for h in range(heads):
            states[h][...] = inputs[h][7][...].astype(F32)

    for h in range(heads):
        q, k, v, d_out, mask, q_decay, k_decay, ignored = inputs[h]
        d_q, d_k, d_v = outputs[h]
        state = states[h]
        do = d_out[...]
        weights = (mm(q[...], k[...], NT) * mask[...]).astype(BF16)
        d_v[...] = mm(weights, do, TN)
        d_scores = mm(do, v[...], NT).astype(BF16).astype(F32)
        d_scores = (d_scores * mask[...]).astype(BF16)
        d_k[...] = mm(d_scores, q[...], TN)
        far = mm(do, state[...].astype(BF16), NT).astype(BF16).astype(F32)
        dq = mm(d_scores, k[...], NN) + far * q_decay[...]
        dq = dq.astype(BF16).astype(F32)
        d_q[...] = turn(dq, cosine[...], -sine[...]).astype(BF16)
        state[...] = params[2 + h] * state[...] + mm(scaled(k[...], k_decay[...]), v[...], TN)


def outer_back_kernel(roles, params, cosine, sine, *refs):
    heads = len(roles)
    counts = [10 + 2 * t.count("g") for t in roles]
    inputs = take(refs, counts)
    outputs = refs[sum(counts) : sum(counts) + heads]
    states = refs[sum(counts) + heads :]

    @pl.when(pl.program_id(0) == 0)
    def _():
        for h in range(heads):
            states[h][...] = inputs[h][9][...].astype(F32)

    other = None
    for h in reversed(range(heads)):
        q, k, v, d_out, d_q, d_k, d_v, q_decay, k_decay, ignored, *gates = inputs[h]
        state = states[h]
        low = state[...].astype(BF16)
        far = mm(v[...], low, NT).astype(BF16).astype(F32)
        dk = (d_k[...] + far * k_decay[...]).astype(BF16).astype(F32)
        dk = turn(dk, cosine[...], -sine[...]).astype(BF16)
        dv = (d_v[...] + mm(scaled(k[...], k_decay[...]), low, NN)).astype(BF16)
        for n, role in enumerate(roles[h]):
            if role == "q":
                value = d_q[...]
            elif role == "k":
                value = dk
            elif role == "va":
                value = dv[:, :DK]
            elif role == "vb":
                value = dv[:, DK:]
            elif role == "xv":
                value = other
            else:
                value = select(params, gates.pop(0), gates.pop(0)).astype(BF16)
            outputs[h][:, n * DK : (n + 1) * DK] = value
        other = dv[:, :DK]
        state[...] = params[2 + h] * state[...] + mm(scaled(q[...], q_decay[...]), d_out[...], TN)


def head_call(kernel, grid, operands, outputs, scratch, flops):
    arrays = [t[0] for t in operands]
    size = sum(t.size * t.dtype.itemsize for t in arrays + [t[0] for t in outputs])
    call = pl.pallas_call(
        kernel,
        grid=(grid,),
        in_specs=[
            pl.BlockSpec(memory_space=pltpu.SMEM) if block is None else pl.BlockSpec(block, where)
            for _, block, where in operands
        ],
        out_specs=[pl.BlockSpec(block, where) for _, block, where in outputs],
        scratch_shapes=scratch,
        out_shape=[t[0] for t in outputs],
        compiler_params=pltpu.CompilerParams(vmem_limit_bytes=56 * 2**20),
        cost_estimate=pl.CostEstimate(flops=flops, bytes_accessed=size, transcendentals=0),
    )
    return list(call(*arrays))


def place_kernel(parts, target, source, *refs):
    out = refs[-1]
    code = source[pl.program_id(1)]
    for i, part in enumerate(parts):

        @pl.when(code == i)
        def _(part=part):
            row = 0
            for n in part:
                piece = refs[n]
                out[row : row + piece.shape[0], :] = piece[...].astype(F32)
                row += piece.shape[0]


def place_blocks(parts, target, source, shape, block, where, outer=1):
    flat, index = [], []
    for part in parts:
        for piece in part:
            if not any(piece is t for t in flat):
                flat.append(piece)
        index.append([next(n for n, t in enumerate(flat) if t is piece) for piece in part])
    return pl.pallas_call(
        functools.partial(place_kernel, index),
        grid_spec=pltpu.PrefetchScalarGridSpec(
            num_scalar_prefetch=2,
            grid=(outer, target.shape[0]),
            in_specs=[
                pl.BlockSpec((t.shape[0], t.shape[1] // outer), lambda o, n, target, source: (0, o))
                for t in flat
            ],
            out_specs=pl.BlockSpec(block, lambda o, n, target, source: where(o, target[n])),
        ),
        out_shape=jax.ShapeDtypeStruct(shape, F32),
        compiler_params=pltpu.CompilerParams(vmem_limit_bytes=48 * 2**20),
    )(target.astype(jnp.int32), source.astype(jnp.int32), *flat)


def local(
    tokens,
    cotangent,
    gain_attn,
    gain_ffn,
    mixer_in,
    mixer_out,
    ffn_in,
    ffn_out,
    segment_order,
    decay_index,
):
    rows, width = tokens.shape
    group = lax.axis_size("seq")
    segments = lax.axis_size("shard")
    heads = decay_index.shape[0]
    local_heads = heads // group
    seg_len = rows * group
    blk = min(512, seg_len)
    blocks = seg_len // blk
    vcols = local_heads * DV
    s = lax.axis_index("seq")
    j = lax.axis_index("shard")

    def swap(v, d):
        return lax.ppermute(v, "seq", [(i, i ^ d) for i in range(group)])

    def cross(v, d):
        return lax.ppermute(v, "shard", [(i, i ^ d) for i in range(segments)])

    def pick(v, i):
        return lax.dynamic_index_in_dim(v, i, 0, keepdims=False)

    def spread(v, beside=None):
        if group == 4:
            h = v.shape[0] // 2
            r1 = swap(v, 1)
            r2 = swap(v, 2)
            if beside is not None:
                r1, r2, beside[:] = tie(r1, r2, list(beside))
            return [(v,), (r1,), (r2,), (swap(r1[:h], 2), swap(r2[h:], 1))]
        return [(v,)] + [(swap(v, d),) for d in range(1, group)]

    def ordered(parts):
        r = parts[0][0].shape[0]
        out = jnp.zeros((group * r,) + parts[0][0].shape[1:], parts[0][0].dtype)
        for d, part in enumerate(parts):
            row = (s ^ d) * r
            for piece in part:
                out = lax.dynamic_update_slice_in_dim(out, piece, row, 0)
                row = row + piece.shape[0]
        return out

    def gather_near(v):
        return jnp.concatenate([piece for part in spread(v) for piece in part], axis=0)

    def gather_seq(v):
        return ordered(spread(v))

    def first_step(blk_of):
        b = [blk_of(d) for d in range(4)]
        h = b[0].shape[0] // 2
        sa = jnp.concatenate([b[1][:h], b[3][:h]], axis=0)
        sb = jnp.concatenate([b[2][h:], b[3][h:]], axis=0)
        sa, sb = tie(sa, sb)
        return b, swap(sa, 1), swap(sb, 2)

    def second_step(b, ra, rb):
        h = b[0].shape[0] // 2
        ra, rb = ra.astype(F32), rb.astype(F32)
        qa = (b[2][:h].astype(F32) + ra[h:]).astype(BF16)
        qb = (b[1][h:].astype(F32) + rb[h:]).astype(BF16)
        qa, qb = tie(qa, qb)
        qa, qb = swap(qa, 2), swap(qb, 1)
        top = b[0][:h].astype(F32) + ra[:h] + qa.astype(F32)
        return jnp.concatenate([top, b[0][h:].astype(F32) + rb[:h] + qb.astype(F32)], axis=0)

    def send_blocks(blk_of):
        sent = tie(*(blk_of(d) for d in range(group)))
        return sent[0], [swap(sent[d], d) for d in range(group - 1, 0, -1)]

    def add_blocks(own, got):
        own = own.astype(F32)
        for t in got:
            own = own + t.astype(F32)
        return own

    def near_rows(v):
        return lambda d: v[d * rows : (d + 1) * rows]

    def seq_rows(v):
        return lambda d: lax.dynamic_slice_in_dim(v, (s ^ d) * rows, rows, 0)

    def gather_shard(v):
        return lax.all_gather(v, "shard", axis=0, tiled=True)

    def reduce_shard(v):
        return lax.psum_scatter(v, "shard", scatter_dimension=0, tiled=True)

    balanced = group == 4 and local_heads == 2 and segments == 8
    units = mixer_in.reshape(-1, DK, width)
    if balanced:
        keep, give, back, lend = (jnp.asarray(t) for t in balanced_tables())
        core = j % 2
    else:
        keep, give, place, held, back, lend = (
            jnp.asarray(t) for t in unit_tables(group, local_heads, segments)
        )

    def offered(h):
        kept, given = keep[h, j, s], give[h, j, s]
        if balanced and h == 1:
            cut = mixer_in.reshape(-1, DK // 2, width)
            own = pick(cut, 2 * jnp.maximum(kept, 0) + core)
            given = cross(pick(cut, 2 * given + 1 - core), 1)
        else:
            own = pick(units, jnp.maximum(kept, 0))
            given = cross(pick(units, given), 1)
        return jnp.where(kept >= 0, own, given)

    sub = ffn_in.shape[0] // group
    ffn_out_cut = ffn_out.reshape(ffn_out.shape[0], segments // 2, group, sub)

    my_rank = jnp.sum(jnp.where(jnp.arange(segments) == j, segment_order, 0))
    all_logs = jnp.log1p(-jnp.exp2(-(5.0 + decay_index.astype(F32))))
    logs = lax.dynamic_index_in_dim(all_logs.reshape(local_heads, group), s, 1, keepdims=False)
    half = DK // 2
    inv_freq = jnp.exp(-jnp.log(10000.0) * jnp.arange(half).astype(F32) / half)
    positions = my_rank * seg_len + jnp.arange(seg_len, dtype=jnp.int32)
    angles = positions.astype(F32)[:, None] * inv_freq[None, :]
    cosine = jnp.cos(angles)
    sine = jnp.sin(angles)
    steps = jnp.arange(blk).astype(F32)
    gap = steps[:, None] - steps[None, :]
    masks = jnp.where(
        gap[None] >= 0.0, jnp.exp(jnp.maximum(gap, 0.0)[None] * logs[:, None, None]), 0.0
    )
    q_decays = jnp.exp((steps + 1.0)[None, :] * logs[:, None])[..., None]
    k_decays = jnp.exp((blk - 1.0 - steps)[None, :] * logs[:, None])[..., None]
    block_decays = jnp.exp(blk * logs)

    xf = tokens.astype(F32)
    normed = gather_seq(rms_scale(xf, gain_attn).astype(BF16))
    d_ffn = gather_near(cotangent)
    slots = [gather_shard(offered(0))]
    slots[0], normed, d_ffn, cosine, sine, masks, q_decays, k_decays = tie(
        slots[0], normed, d_ffn, cosine, sine, masks, q_decays, k_decays
    )
    for h in range(1, local_heads):
        slots.append(gather_shard(offered(h)))
    mixer_out_cut = jnp.concatenate(
        [
            lax.dynamic_slice_in_dim(mixer_out, (h * group + s) * DV, DV, 1)
            for h in range(local_heads)
        ],
        axis=1,
    )
    mixer_out_cut, slots[0] = tie(mixer_out_cut, slots[0])
    w_out = gather_shard(mixer_out_cut)
    later = [
        lax.dynamic_slice_in_dim(ffn_in, s * sub, sub, 0),
        lax.dynamic_index_in_dim(ffn_out_cut, s, 2, keepdims=False).reshape(ffn_out.shape[0], -1),
    ]
    inner_cols = later[1].shape[1]

    ranks = segment_order
    piece = DK // segments

    def exchange_states(hs, totals, reverse, beside=()):
        cut = jnp.concatenate([t.reshape(segments, piece, DV) for t in totals], axis=1)
        got = lax.all_to_all(cut, "shard", split_axis=0, concat_axis=0, tiled=True)
        got, *beside = tie(got, *beside)
        apart = ranks[:, None] - ranks[None, :] - 1
        if reverse:
            apart = -apart - 2
        distance = apart.astype(F32)
        joined = []
        for n, h in enumerate(hs):
            coef = jnp.where(
                distance >= 0.0, jnp.exp(jnp.maximum(distance, 0.0) * seg_len * logs[h]), 0.0
            )
            part = got[:, n * piece : (n + 1) * piece].astype(F32)
            joined.append(jnp.sum(coef[..., None, None] * part[None], axis=1).astype(BF16))
        joined = jnp.concatenate(joined, axis=1)
        back_cut = lax.all_to_all(joined, "shard", split_axis=0, concat_axis=0, tiled=True)
        states = [
            back_cut[:, n * piece : (n + 1) * piece].reshape(DK, DV) for n in range(len(hs))
        ]
        return (states, *beside)

    def whole(n):
        return (0, 0)

    def ahead(n):
        return (n, 0)

    def behind(n):
        return (blocks - 1 - n, 0)

    def shaped(columns, kind, r=seg_len):
        return jax.ShapeDtypeStruct((r, columns), kind)

    state_scratch = [pltpu.VMEM((DK, DV), F32)]
    half_block = (blk, half)
    unit_block, v_block = (blk, DK), (blk, DV)
    ret_flops = 2 * seg_len * (DK + DV) * (blk + DK)
    low = s < group // 2
    if balanced:
        roles = [["q", "k", "va", "vb", "xv", "g", "g", "g"], ["q", "k", "vb", "g"]]
    else:
        roles = [["q", "k", "va", "vb", "g", "g"]] * local_heads
    params = [
        (jnp.stack([block_decays[h], low.astype(F32)]), None, None) for h in range(local_heads)
    ]
    heads_kept = []
    extra_v = None
    for h in range(local_heads):
        if balanced:
            weights = slots[h]
        else:
            cut = slots[h].reshape(-1, DK, width)
            weights = jnp.concatenate([pick(cut, place[h, s, c]) for c in range(6)], axis=0)
        carried = "va" not in roles[h]
        gate_count = roles[h].count("g")
        q, k, v, total, gates, *extra = head_call(
            functools.partial(project_kernel, blk, roles[h], carried),
            len(roles[h]) // 2,
            [
                params[h],
                (normed, (seg_len, width), whole),
                (weights, (2 * DK, width), ahead),
                (cosine, (seg_len, half), whole),
                (sine, (seg_len, half), whole),
                (k_decays[h], (blk, 1), whole),
            ]
            + ([(extra_v, (seg_len, DK), whole)] if carried else []),
            [
                (shaped(DK, BF16), (seg_len, DK), whole),
                (shaped(DK, BF16), (seg_len, DK), whole),
                (shaped(DV, BF16), (seg_len, DV), whole),
                (shaped(DV, BF16, DK), (DK, DV), whole),
                (shaped(gate_count * DK, BF16), (seg_len, gate_count * DK), whole),
            ]
            + ([(shaped(DK, BF16), (seg_len, DK), whole)] if "xv" in roles[h] else []),
            [pltpu.VMEM((seg_len, 2 * DK), F32)],
            2 * seg_len * width * len(roles[h]) * DK,
        )
        extra_v = extra[0] if extra else None
        (state_in,) = exchange_states([h], [total], False)[0]
        if h + 1 < local_heads:
            slots[h + 1], state_in, *later[:] = tie(slots[h + 1], state_in, *later)
        heads_kept.append((weights, q, k, v, gates, state_in))

    def columns(v, c, order):
        return (v, unit_block, lambda n, c=c: (order(n)[0], c))

    if balanced:
        gates0, gates1 = heads_kept[0][4], heads_kept[1][4]
        swapped = swap(jnp.where(low, gates1, gates0[:, :DK]), 2)

        def gate_operands(h, order):
            if h == 0:
                four = (gates0, 0), (gates0, 1), (swapped, 0), (gates0, 2)
            else:
                four = (gates0, 1), (gates1, 0), (gates0, 2), (swapped, 0)
            return [columns(v, c, order) for v, c in four]

    else:

        def gate_operands(h, order):
            return [columns(heads_kept[h][4], c, order) for c in (0, 0, 1, 1)]

    kept = []
    for h in range(local_heads):
        weights, q, k, v, gates, state_in = heads_kept[h]
        hidden, mixed, retained = head_call(
            retain_kernel,
            blocks,
            [
                params[h],
                (q, unit_block, ahead),
                (k, unit_block, ahead),
                (v, v_block, ahead),
                *gate_operands(h, ahead),
                (masks[h], (blk, blk), whole),
                (q_decays[h], (blk, 1), whole),
                (k_decays[h], (blk, 1), whole),
                (state_in, (DK, DV), whole),
            ],
            [
                (shaped(DV, BF16), v_block, ahead),
                (shaped(DV, BF16), v_block, ahead),
                (shaped(1, F32), (blk, 1), ahead),
            ],
            state_scratch,
            ret_flops,
        )
        kept.append((retained, mixed, hidden))
    hidden = jnp.concatenate([t[-1] for t in kept], axis=1)
    w_ffn_in, w_ffn_out = (gather_shard(t) for t in later)

    resid = xf + add_blocks(*send_blocks(seq_rows(dot_nt(hidden, w_out, BF16))))
    normed2 = gather_near(rms_scale(resid, gain_ffn).astype(BF16))
    proj2 = dot_nt(normed2, w_ffn_in)
    first, second = proj2[:, :inner_cols], proj2[:, inner_cols:]
    inner2 = gated_gelu(first, second).astype(BF16)

    g_ffn_out, d_ffn = tie(dot_tn(d_ffn, inner2, BF16), d_ffn)
    scattered = {"ffn_out": reduce_shard(g_ffn_out)}
    d_inner2 = dot_nn(d_ffn, w_ffn_out)
    ignored2, gelu_back = jax.vjp(gated_gelu, first, second)
    d_first, d_second = gelu_back(d_inner2)
    dproj2 = jnp.concatenate([d_first, d_second], axis=1).astype(BF16)
    d_normed2 = dot_nn(dproj2, w_ffn_in, BF16)
    g_ffn_in = dot_tn(dproj2, normed2, BF16)
    if group == 4:
        terms, ra, rb = first_step(near_rows(d_normed2))
        ra, rb, g_ffn_in = tie(ra, rb, g_ffn_in)
        d_normed2 = second_step(terms, ra, rb)
    else:
        d_normed2 = add_blocks(*send_blocks(near_rows(d_normed2)))
    scattered["ffn_in"] = reduce_shard(g_ffn_in)
    ignored3, norm2_back = jax.vjp(rms_scale, resid, gain_ffn)
    d_resid_part, d_gain_ffn = norm2_back(d_normed2)
    d_resid = cotangent.astype(F32) + d_resid_part
    (d_attn,) = tie(d_resid.astype(BF16))
    d_attn = gather_seq(d_attn)
    d_attn, scattered["ffn_out"] = tie(d_attn, scattered["ffn_out"])
    parts_ffn_out = spread(scattered["ffn_out"])

    def tie_parts(v, parts):
        flat = tie(v, *(piece for part in parts for piece in part))
        rest = list(flat[1:])
        return flat[0], [tuple(rest.pop(0) for _ in part) for part in parts]

    all_params = (
        jnp.concatenate([jnp.stack([jnp.float32(0.0), low.astype(F32)]), block_decays]),
        None,
        None,
    )
    outs = head_call(
        functools.partial(gate_back_kernel, local_heads),
        blocks,
        [
            all_params,
            (d_attn, (blk, width), behind),
            (w_out, (width, vcols), whole),
        ]
        + [
            t
            for h in range(local_heads)
            for t in (
                *gate_operands(h, behind),
                (kept[h][1], v_block, behind),
                (kept[h][0], (blk, 1), behind),
                (heads_kept[h][1], unit_block, behind),
                (q_decays[h], (blk, 1), whole),
            )
        ],
        [
            (shaped(DV, BF16), v_block, behind),
            (shaped(DV, BF16), v_block, behind),
            (shaped(DV, BF16, DK), (DK, DV), whole),
        ]
        * local_heads,
        state_scratch * local_heads,
        2 * seg_len * (DK * DV * local_heads + width * vcols),
    )
    d_gates, d_outs, totals = outs[0::3], outs[1::3], outs[2::3]
    if balanced:
        d_swapped = swap(jnp.where(low, d_gates[0][:, DK:], d_gates[1][:, DK:]), 2)
    else:
        d_swapped = totals[0]
    if group == 4:
        totals[0], parts_ffn_out[:3] = tie_parts(totals[0], parts_ffn_out[:3])
    hidden, totals[0] = tie(hidden, totals[0])
    g_mixer_out = dot_tn(d_attn, hidden, BF16)
    inners = head_call(
        functools.partial(inner_back_kernel, local_heads),
        blocks,
        [all_params, (cosine, half_block, ahead), (sine, half_block, ahead)]
        + [
            t
            for h in range(local_heads)
            for t in (
                (heads_kept[h][1], unit_block, ahead),
                (heads_kept[h][2], unit_block, ahead),
                (heads_kept[h][3], v_block, ahead),
                (d_outs[h], v_block, ahead),
                (masks[h], (blk, blk), whole),
                (q_decays[h], (blk, 1), whole),
                (k_decays[h], (blk, 1), whole),
                (heads_kept[h][5], (DK, DV), whole),
            )
        ],
        [
            (shaped(DK, BF16), unit_block, ahead),
            (shaped(DK, F32), unit_block, ahead),
            (shaped(DV, F32), v_block, ahead),
        ]
        * local_heads,
        state_scratch * local_heads,
        2 * local_heads * ret_flops,
    )
    flat_ffn_out = [piece for part in parts_ffn_out for piece in part]
    grads_out, d_swapped, g_mixer_out, inner2, scattered["ffn_in"], *flat = exchange_states(
        range(local_heads),
        totals,
        True,
        (d_swapped, g_mixer_out, inner2, scattered["ffn_in"], *inners, *flat_ffn_out),
    )
    scattered["mixer_out"] = reduce_shard(g_mixer_out)
    inners = flat[: 3 * local_heads]
    rest = flat[3 * local_heads :]
    parts_ffn_out = [tuple(rest.pop(0) for _ in part) for part in parts_ffn_out]
    parts_ffn_in = spread(scattered["ffn_in"])
    near = jnp.arange(group)
    if sub % 128 == 0:
        g_ffn_out = place_blocks(
            parts_ffn_out,
            s ^ near,
            near,
            ffn_out.shape,
            (ffn_out.shape[0], sub),
            lambda o, n: (0, o * group + n),
            outer=segments // 2,
        )
    else:
        g_ffn_out = jnp.transpose(
            ordered(parts_ffn_out).reshape(group, ffn_out.shape[0], segments // 2, sub),
            (1, 2, 0, 3),
        ).reshape(ffn_out.shape).astype(F32)
    ffn_terms, g_ffn_out, *grads_out = tie(
        dot_nt(inner2, w_ffn_out, BF16), g_ffn_out, *grads_out
    )
    if balanced:
        d_gate_pairs = [
            [
                ((d_gates[0], 0), (d_swapped, 0)),
                ((d_gates[1], 0), (d_gates[0], 0)),
                ((d_gates[1], 1), (d_gates[0], 1)),
            ],
            [((d_swapped, 0), (d_gates[1], 0))],
        ]
    else:
        d_gate_pairs = [[((t, 0), (t, 0)), ((t, 1), (t, 1))] for t in d_gates]
    by_units = head_call(
        functools.partial(outer_back_kernel, roles),
        blocks,
        [all_params, (cosine, half_block, behind), (sine, half_block, behind)]
        + [
            t
            for h in range(local_heads)
            for t in (
                (heads_kept[h][1], unit_block, behind),
                (heads_kept[h][2], unit_block, behind),
                (heads_kept[h][3], v_block, behind),
                (d_outs[h], v_block, behind),
                (inners[3 * h], unit_block, behind),
                (inners[3 * h + 1], unit_block, behind),
                (inners[3 * h + 2], v_block, behind),
                (q_decays[h], (blk, 1), whole),
                (k_decays[h], (blk, 1), whole),
                (grads_out[h], (DK, DV), whole),
                *(columns(v, c, behind) for pair in d_gate_pairs[h] for v, c in pair),
            )
        ],
        [(shaped(len(t) * DK, BF16), (blk, len(t) * DK), behind) for t in roles],
        state_scratch * local_heads,
        seg_len * DK * DV,
    )

    if group == 4:
        late = first_step(near_rows(ffn_terms))
    else:
        late = send_blocks(near_rows(ffn_terms))
    by_units[0], parts_ffn_in[:3] = tie_parts(by_units[0], parts_ffn_in[:3])
    g_units = [dot_tn(by_units[0], normed, BF16)]
    by_units[-1], g_units[0] = tie(by_units[-1], g_units[0])
    by_units[-1], scattered["mixer_out"] = tie(by_units[-1], scattered["mixer_out"])
    tile = 512
    rights = [t[0] for t in heads_kept]
    (d_normed,) = head_call(
        functools.partial(join_kernel, local_heads),
        width // tile,
        [(t, t.shape, whole) for t in by_units]
        + [(t, (t.shape[0], tile), lambda n: (0, n)) for t in rights],
        [(shaped(width, BF16), (seg_len, tile), lambda n: (0, n))],
        [],
        seg_len * width,
    )
    d_normed, parts_ffn_in = tie_parts(d_normed, parts_ffn_in)
    if group == 4:
        ffn_own, ra, rb = late
        d_normed, ra, rb = tie(d_normed, ra, rb)
        first = first_step(seq_rows(d_normed))
        output = (resid + second_step(ffn_own, ra, rb)).astype(BF16)
    else:
        output = (resid + add_blocks(*late)).astype(BF16)
    parts_mixer_out = spread(scattered["mixer_out"])
    for h in range(1, local_heads):
        by_units[h], d_normed = tie(by_units[h], d_normed)
        g_units.append(dot_tn(by_units[h], normed, BF16))
    g_ffn_in = place_blocks(
        parts_ffn_in, s ^ near, near, ffn_in.shape, (sub, width), lambda o, n: (n, 0)
    )
    if group == 4:
        own, ra, rb = first
        ra, rb, g_units[-1], g_ffn_in = tie(ra, rb, g_units[-1], g_ffn_in)
        d_normed = second_step(own, ra, rb)
    else:
        d_normed = add_blocks(*send_blocks(seq_rows(d_normed)))
    g_slots = []
    for h in range(local_heads):
        if not balanced:
            cut = g_units[h].reshape(-1, DK, width)
            g_units[h] = jnp.concatenate(
                [pick(cut, jnp.maximum(held[h, c, s], 0)) for c in range(segments)], axis=0
            )
        g_slots.append(reduce_shard(g_units[h]))

    ignored8, norm1_back = jax.vjp(rms_scale, xf, gain_attn)
    d_x_part, d_gain_attn = norm1_back(d_normed)
    input_grad = (d_resid + d_x_part).astype(BF16)
    gains = jnp.concatenate([d_gain_attn, d_gain_ffn])[None]
    step = 1
    while step < group:
        gains = gains + swap(gains, step)
        step *= 2
    g_slots[0], gains = tie(g_slots[0], gains)
    gains = lax.all_to_all(
        jnp.broadcast_to(gains, (segments, 2 * width)),
        "shard",
        split_axis=0,
        concat_axis=0,
        tiled=True,
    )
    gains = jnp.sum(gains, axis=0)
    parts = []
    for h in range(local_heads):
        last = h == local_heads - 1
        beside = None
        if h == 0:
            g_slots[h], input_grad = tie(g_slots[h], input_grad)
            g_slots[h], parts_mixer_out = tie_parts(g_slots[h], parts_mixer_out)
            g_mixer_out = place_blocks(
                parts_mixer_out,
                s ^ near,
                near,
                mixer_out.shape,
                (mixer_out.shape[0], DV),
                lambda o, n: (0, o * group + n),
                outer=local_heads,
            )
            beside = [g_mixer_out, output, gains]
        if last and h > 0:
            g_slots[h], gains, g_mixer_out = tie(g_slots[h], gains, g_mixer_out)
            g_slots[h], parts = tie_parts(g_slots[h], parts)
        here = spread(g_slots[h], beside)
        if group == 4 and h == 0:
            g_mixer_out, output, gains = beside
        if balanced and last:
            there = [tuple(cross(piece, 1) for piece in part) for part in here]
            parts += [a + b for a, b in zip(here, there)] + [b + a for a, b in zip(here, there)]
        else:
            lend_here = lend[j] if balanced else lend[h, j]
            stack = jnp.stack([jnp.concatenate(part, axis=0) for part in here])
            parts += here + [
                (cross(pick(stack, s ^ lend_here[n]), 1),) for n in range(lend_here.shape[0])
            ]
    gain_attn_grad, gain_ffn_grad = gains[:width], gains[width:]
    found = back[j]
    if balanced:
        spare = lend.shape[-1]
        source = jnp.where(
            found[:, 0] == 0,
            s ^ found[:, 1],
            jnp.where(
                found[:, 0] == 1,
                group + found[:, 1],
                group + spare + core * group + (s ^ found[:, 1]),
            ),
        )
    else:
        source = found[:, 0] * (group + lend.shape[-1]) + jnp.where(
            found[:, 2] < 0, s ^ found[:, 1], group + found[:, 2]
        )
    g_mixer_in = place_blocks(
        parts,
        jnp.arange(source.shape[0]),
        source,
        mixer_in.shape,
        (DK, width),
        lambda o, n: (n, 0),
    )
    return (
        output,
        input_grad,
        gain_attn_grad,
        gain_ffn_grad,
        g_mixer_in,
        g_mixer_out,
        g_ffn_in,
        g_ffn_out,
    )


def solution(mesh):
    return jax.shard_map(
        local,
        mesh=mesh,
        in_specs=(
            P(("shard", "seq"), None),
            P(("shard", "seq"), None),
            P(),
            P(),
            P("shard", None),
            P("shard", None),
            P("shard", None),
            P("shard", None),
            P(),
            P(),
        ),
        out_specs=(
            P(("shard", "seq"), None),
            P(("shard", "seq"), None),
            P(),
            P(),
            P("shard", None),
            P("shard", None),
            P("shard", None),
            P("shard", None),
        ),
        check_vma=False,
    )
```

profile of v0, /device:TPU:0, one launch (start us, length us, event | category | flops | bytes accessed | tf_op | source)
XLA Modules:
  0.0 765.3 jit_solution(15059783916189671312)
XLA Ops:
  43.2 11.2 %collective-permute-done.1 = bf16[256,2048]{1,0:T(8,128)(2,1)} collective-permute-done((bf16[256,2048]{1,0:T(8,128)(2,1)}, bf16[256,2048]{1,0:T(8,128)(2,1)}, u32[]{:S(2)}, u32[]{:S(2)}) %collective-permute-start.1) | collective-permute-done | bytes 1048608 | tf_op jit(solution)/shard_map/ppermute | solution.py:428
  60.3 16.6 %collective-permute-done.5 = bf16[256,2048]{1,0:T(8,128)(2,1)} collective-permute-done((bf16[256,2048]{1,0:T(8,128)(2,1)S(1)}, bf16[256,2048]{1,0:T(8,128)(2,1)}, u32[]{:S(2)}, u32[]{:S(2)}) %collective-permute-start.5) | collective-permute-done | bytes 1048608 | tf_op jit(solution)/shard_map/ppermute | solution.py:428
  92.1 8.1 %collective-permute-done.7 = bf16[128,2048]{1,0:T(8,128)(2,1)S(1)} collective-permute-done((bf16[128,2048]{1,0:T(8,128)(2,1)S(1)}, bf16[128,2048]{1,0:T(8,128)(2,1)S(1)}, u32[]{:S(2)}, u32[]{:S(2)}) %collective-permute-start.7) | collective-permute-done | bytes 524320 | tf_op jit(solution)/shard_map/ppermute | solution.py:428
  107.0 16.3 %shard_map.197 = (bf16[1024,256]{1,0:T(8,128)(2,1)}, bf16[1024,256]{1,0:T(8,128)(2,1)}, bf16[1024,512]{1,0:T(8,128)(2,1)}, bf16[256,512]{1,0:T(8,128)(2,1)}, bf1...) custom-call(f32[2]{0:T(128)} %get-tuple-element.376.params, bf16[1024,2048]{1,0:T(8,128)(2,1)} %constant_dynamic-update-slice_fusion.17.x, ...), custom_call_target="tpu_custom_call" | custom-call | flops 8589934592 | bytes 18089992 | tf_op jit(solution)/shard_map/pallas_call | solution.py:363
  130.8 14.5 %all-to-all-done = bf16[8,32,512]{2,1,0:T(8,128)(2,1)S(1)} async-done(((bf16[8,32,512]{2,1,0:T(8,128)(2,1)}), bf16[8,32,512]{2,1,0:T(8,128)(2,1)S(1)}, u32[]{:S(2)}, u32[]{:S(2)}) %all-to-all-start) | async-done | bytes 262176 | tf_op jit(solution)/shard_map/all_to_all | solution.py:573
  159.7 10.7 %shard_map.198 = (bf16[1024,256]{1,0:T(8,128)(2,1)}, bf16[1024,256]{1,0:T(8,128)(2,1)}, bf16[1024,512]{1,0:T(8,128)(2,1)}, bf16[256,512]{1,0:T(8,128)(2,1)}, bf16[1024,256]{1,0:T(8,128)(2,1)}) custom-call(f32[2]{0:T(128)} %get-tuple-element.377.params, bf16[1024,2048]{1,0:T(8,128)(2,1)} %constant_dynamic-update-slice_fusion.17.x, ...), custom_call_target="tpu_custom_call" | custom-call | flops 4294967296 | bytes 12847112 | tf_op jit(solution)/shard_map/pallas_call | solution.py:363
  180.3 11.3 %all-to-all-done.2 = bf16[8,32,512]{2,1,0:T(8,128)(2,1)S(1)} async-done(((bf16[8,32,512]{2,1,0:T(8,128)(2,1)}), bf16[8,32,512]{2,1,0:T(8,128)(2,1)S(1)}, u32[]{:S(2)}, u32[]{:S(2)}) %all-to-all-start.2) | async-done | bytes 262176 | tf_op jit(solution)/shard_map/all_to_all | solution.py:573
  221.4 7.4 convolution_convert_fusion.7
  234.0 23.7 %collective-permute-done.11 = bf16[256,2048]{1,0:T(8,128)(2,1)} collective-permute-done((bf16[256,2048]{1,0:T(8,128)(2,1)}, bf16[256,2048]{1,0:T(8,128)(2,1)}, u32[]{:S(2)}, u32[]{:S(2)}) %collective-permute-start.11) | collective-permute-done | bytes 1048608 | tf_op jit(solution)/shard_map/ppermute | solution.py:428
  257.8 21.4 %collective-permute-done.12 = bf16[256,2048]{1,0:T(8,128)(2,1)} collective-permute-done((bf16[256,2048]{1,0:T(8,128)(2,1)S(1)}, bf16[256,2048]{1,0:T(8,128)(2,1)}, u32[]{:S(2)}, u32[]{:S(2)}) %collective-permute-start.12) | collective-permute-done | bytes 1048608 | tf_op jit(solution)/shard_map/ppermute | solution.py:428
  285.6 23.1 %collective-permute-done.14 = bf16[256,2048]{1,0:T(8,128)(2,1)S(1)} collective-permute-done((bf16[256,2048]{1,0:T(8,128)(2,1)S(1)}, bf16[256,2048]{1,0:T(8,128)(2,1)S(1)}, u32[]{:S(2)}, u32[]{:S(2)}) %collective-permute-start.14) | collective-permute-done | bytes 1048608 | tf_op jit(solution)/shard_map/ppermute | solution.py:428
  313.0 8.9 %collective-permute-done.16 = bf16[128,2048]{1,0:T(8,128)(2,1)S(1)} collective-permute-done((bf16[128,2048]{1,0:T(8,128)(2,1)S(1)}, bf16[128,2048]{1,0:T(8,128)(2,1)S(1)}, u32[]{:S(2)}, u32[]{:S(2)}) %collective-permute-start.16) | collective-permute-done | bytes 524320 | tf_op jit(solution)/shard_map/ppermute | solution.py:428
  323.5 12.6 %fusion.48 = f32[1024,2048]{1,0:T(8,128)S(1)} fusion(bf16[1024,2048]{1,0:T(8,128)(2,1)} %constant_dynamic-update-slice_fusion.7, bf16[2048,2048]{1,0:T(8,128)(2,1)} %all-gather.12.cloned.1.call-done), kind=kOutput, calls=%fused_computation.194 | convolution fusion | flops 8589934592 | bytes 20971520 | tf_op jit(solution)/shard_map/dot_general | solution.py:26
  348.2 12.6 %fusion.6 = (bf16[1024,1024]{1,0:T(8,128)(2,1)S(1)}, bf16[1024,1024]{1,0:T(8,128)(2,1)S(1)}) fusion(f32[1024,2048]{1,0:T(8,128)} %copy-done.10, bf16[1024,2048]{1,0:T(8,128)(2,1)} %constant_dynamic-update-slice_fusion, bf16[2048,1024]{0,1:T(8,128)(2,1)} %all-gather.14.cloned.1.call-done), kind=kOutput, calls=%fused_computation.10 | convolution fusion | flops 4320133120 | bytes 20971520 | tf_op jit(solution)/shard_map/dot_general | solution.py:32
  360.8 11.4 %convolution_convert_fusion.2 = bf16[1024,2048]{1,0:T(8,128)(2,1)S(1)} fusion(bf16[2048,2048]{1,0:T(8,128)(2,1)} %all-gather.12.cloned.1.call-done, bf16[1024,1024]{1,0:T(8,128)(2,1)S(1)} %get-tuple-element.309, bf16[1024,1024]{1,0:T(8,128)(2,1)S(1)} %get-tuple-element.308), kind=kOutput, calls=%fused_computation.25 | convolution fusion | flops 8600420352 | bytes 16777216 | tf_op jit(solution)/shard_map/dot_general | solution.py:32
  376.6 14.2 %convolution_convert_fusion.1 = bf16[2048,2048]{1,0:T(8,128)(2,1)} fusion(bf16[1024,2048]{1,0:T(8,128)(2,1)} %constant_dynamic-update-slice_fusion.7, bf16[1024,1024]{1,0:T(8,128)(2,1)S(1)} %get-tuple-element.309, bf16[1024,1024]{1,0:T(8,128)(2,1)S(1)} %get-tuple-element.308), kind=kOutput, calls=%fused_computation.1 | convolution fusion | flops 8602517504 | bytes 16777216 | tf_op jit(solution)/shard_map/dot_general | solution.py:38
  403.7 8.4 %collective-permute-done.20 = bf16[128,2048]{1,0:T(8,128)(2,1)S(1)} collective-permute-done((bf16[128,2048]{1,0:T(8,128)(2,1)S(1)}, bf16[128,2048]{1,0:T(8,128)(2,1)S(1)}, u32[]{:S(2)}, u32[]{:S(2)}) %collective-permute-start.20) | collective-permute-done | bytes 524320 | tf_op jit(solution)/shard_map/ppermute | solution.py:428
  419.2 18.2 %collective-permute-done.22 = bf16[256,2048]{1,0:T(8,128)(2,1)S(1)} collective-permute-done((bf16[256,2048]{1,0:T(8,128)(2,1)S(1)}, bf16[256,2048]{1,0:T(8,128)(2,1)S(1)}, u32[]{:S(2)}, u32[]{:S(2)}) %collective-permute-start.22) | collective-permute-done | bytes 1048608 | tf_op jit(solution)/shard_map/ppermute | solution.py:428
  454.5 13.3 %shard_map.201 = (bf16[1024,512]{1,0:T(8,128)(2,1)}, bf16[1024,512]{1,0:T(8,128)(2,1)}, bf16[256,512]{1,0:T(8,128)(2,1)}, bf16[1024,512]{1,0:T(8,128)(2,1)}, bf1...) custom-call(f32[4]{0:T(128)} %pad_maximum_fusion.16.params, ...), custom_call_target="tpu_custom_call" | custom-call | flops 4831838208 | bytes 25702416 | tf_op jit(solution)/shard_map/pallas_call | solution.py:363
  470.6 11.6 %shard_map.202 = (bf16[1024,256]{1,0:T(8,128)(2,1)}, f32[1024,256]{1,0:T(8,128)}, f32[1024,512]{1,0:T(8,128)}, bf16[1024,256]{1,0:T(8,128)(2,1)}, f32[1024,256]{1,0:T(8,128)}, /*index=5*/f32[1024,512]{1,0:T(8,128)}) custom-call(f32[4]{0:T(128)} %pad_maximum_fusion.16.params, f32[1024,128]{1,0:T(8,128)} %get-tuple-element.151.cosine, ...), custom_call_target="tpu_custom_call" | custom-call | flops 4831838208 | bytes 17309712 | tf_op jit(solution)/shard_map/pallas_call | solution.py:363
  490.5 9.4 %convolution_convert_fusion.5 = bf16[2048,1024]{1,0:T(8,128)(2,1)} fusion(bf16[1024,2048]{1,0:T(8,128)(2,1)} %constant_dynamic-update-slice_fusion.12.d_attn, bf16[1024,1024]{1,0:T(8,128)(2,1)} %copy-done.31), kind=kOutput, calls=%fused_computation.28 | convolution fusion | flops 4297064448 | bytes 10485760 | tf_op jit(solution)/shard_map/dot_general | solution.py:38
  527.8 9.0 %all-to-all-done.5 = bf16[8,64,512]{2,1,0:T(8,128)(2,1)} async-done(((bf16[8,64,512]{2,1,0:T(8,128)(2,1)}), bf16[8,64,512]{2,1,0:T(8,128)(2,1)}, u32[]{:S(2)}, u32[]{:S(2)}) %all-to-all-start.5) | async-done | bytes 524320 | tf_op jit(solution)/shard_map/all_to_all | solution.py:587
  538.7 11.4 %shard_map.204 = (bf16[1024,2048]{1,0:T(8,128)(2,1)}, bf16[1024,1024]{1,0:T(8,128)(2,1)}) custom-call(f32[4]{0:T(128)} %pad_maximum_fusion.16.params, f32[1024,128]{1,0:T(8,128)} %get-tuple-element.151.cosine, f32[1024,128]{1,0:T(8,128)} %get-tuple-element.152.sine, bf16[1024,256]{1,0:T(8,128)(2,1)} %get-tuple-element.157.q.refs_6_.refs_0_, ...), custom_call_target="tpu_custom_call" | custom-call | flops 134217728 | bytes 28844048 | tf_op jit(solution)/shard_map/pallas_call | solution.py:363
  550.1 14.1 %convolution_convert_fusion = bf16[2048,2048]{1,0:T(8,128)(2,1)} fusion(bf16[1024,2048]{1,0:T(8,128)(2,1)} %get-tuple-element.234.refs_0_, bf16[1024,2048]{1,0:T(8,128)(2,1)} %constant_dynamic-update-slice_fusion.17.x), kind=kOutput, calls=%fused_computation | convolution fusion | flops 8594128896 | bytes 16777216 | tf_op jit(solution)/shard_map/dot_general | solution.py:38
  574.0 18.6 %shard_map.205 = bf16[1024,2048]{1,0:T(8,128)(2,1)} custom-call(bf16[1024,2048]{1,0:T(8,128)(2,1)} %get-tuple-element.234.refs_0_, bf16[1024,1024]{1,0:T(8,128)(2,1)} %get-tuple-element.249.refs_1_, bf16[2048,2048]{1,0:T(8,128)(2,1)} %all-gather.6.cloned.1.call-done.w.refs_2_, bf16[1024,2048]{1,0:T(8,128)(2,1)} %all-gather.8.cloned.1.call-done.w.refs_3_), custom_call_target="tpu_custom_call" | custom-call | flops 2097152 | bytes 23068672 | tf_op jit(solution)/shard_map/pallas_call | solution.py:363
  592.6 12.7 %collective-permute-done.33.refs_3_ = bf16[128,2048]{1,0:T(8,128)(2,1)S(1)} collective-permute-done((bf16[128,2048]{1,0:T(8,128)(2,1)}, bf16[128,2048]{1,0:T(8,128)(2,1)S(1)}, u32[]{:S(2)}, u32[]{:S(2)}) %collective-permute-start.33) | collective-permute-done | bytes 524320 | tf_op jit(solution)/shard_map/ppermute | solution.py:428
  617.0 8.4 %convolution_convert_fusion.3 = bf16[1024,2048]{1,0:T(8,128)(2,1)} fusion(bf16[1024,1024]{1,0:T(8,128)(2,1)S(1)} %copy-done.26, bf16[1024,2048]{1,0:T(8,128)(2,1)} %constant_dynamic-update-slice_fusion.17.x), kind=kOutput, calls=%fused_computation.26 | convolution fusion | flops 4297064448 | bytes 10485760 | tf_op jit(solution)/shard_map/dot_general | solution.py:38
  625.3 7.7 %collective-permute-done.37 = bf16[256,2048]{1,0:T(8,128)(2,1)} collective-permute-done((bf16[256,2048]{1,0:T(8,128)(2,1)}, bf16[256,2048]{1,0:T(8,128)(2,1)}, u32[]{:S(2)}, u32[]{:S(2)}) %collective-permute-start.37) | collective-permute-done | bytes 1048608 | tf_op jit(solution)/shard_map/ppermute | solution.py:428
  651.7 7.5 collective-permute-done.39
  662.6 11.0 %collective-permute-done.41 = f32[1,4096]{1,0:T(1,128)S(1)} collective-permute-done((f32[1,4096]{1,0:T(1,128)S(1)}, f32[1,4096]{1,0:T(1,128)S(1)}, u32[]{:S(2)}, u32[]{:S(2)}) %collective-permute-start.41) | collective-permute-done | bytes 16416 | tf_op jit(solution)/shard_map/ppermute | solution.py:428
  726.8 11.4 %collective-permute-done.57.refs_10_ = bf16[128,2048]{1,0:T(8,128)(2,1)S(1)} collective-permute-done((bf16[128,2048]{1,0:T(8,128)(2,1)}, bf16[128,2048]{1,0:T(8,128)(2,1)S(1)}, u32[]{:S(2)}, u32[]{:S(2)}) %collective-permute-start.57) | collective-permute-done | bytes 524320 | tf_op jit(solution)/shard_map/ppermute | solution.py:428
  749.6 8.6 %shard_map.208 = f32[1536,2048]{1,0:T(8,128)} custom-call(s32[6]{0:T(128)S(1)} %iota.50.target, s32[6]{0:T(128)S(1)} %bitcast_select_fusion.3.source, bf16[256,2048]{1,0:T(8,128)(2,1)} %reduce-scatter.10.cloned.1.call-done.refs_0_, bf16[256,2048]{1,0:T(8,128)(2,1)} %copy-done.14, bf16[256,2048]{1,0:T(8,128)(2,1)} %collective-permute-done.48.refs_2_, ...), custom_call_target="tpu_custom_call" | custom-call | tf_op jit(solution)/shard_map/pallas_call | solution.py:387
  (394 shorter events, 335.5 us)
Async XLA Ops:
  7.2 96.4 %all-gather.6.cloned.1.call-start = ((), (), s32[]{:S(2)}) async-start(), calls=%async_computation.12 | async-start | bytes 9437184 | tf_op jit(solution)/shard_map/all_gather | solution.py:497
  16.9 139.6 %all-gather.8.cloned.1.call-start = ((), (), s32[]{:S(2)}) async-start(), calls=%async_computation.13 | async-start | bytes 4718592 | tf_op jit(solution)/shard_map/all_gather | solution.py:497
  22.7 197.4 %all-gather.10.cloned.1.call-start = ((), (), s32[]{:S(2)}) async-start(), calls=%async_computation.14 | async-start | bytes 4718592 | tf_op jit(solution)/shard_map/all_gather | solution.py:497
  27.3 27.1 %collective-permute-start.1 = (bf16[256,2048]{1,0:T(8,128)(2,1)}, bf16[256,2048]{1,0:T(8,128)(2,1)}, u32[]{:S(2)}, u32[]{:S(2)}) collective-permute-start(bf16[256,2048]{1,0:T(8,128)(2,1)} %get-tuple-element.305), channel_id=1, source_target_pairs={{0,8},{8,0},{16,24},{24,16},{1,9},{9,1},{17,25},{25,17},{2,10},{10... | collective-permute-start | bytes 3145736 | tf_op jit(solution)/shard_map/ppermute | solution.py:428
  30.1 27.5 %collective-permute-start.2 = (bf16[256,2048]{1,0:T(8,128)(2,1)}, bf16[256,2048]{1,0:T(8,128)(2,1)}, u32[]{:S(2)}, u32[]{:S(2)}) collective-permute-start(bf16[256,2048]{1,0:T(8,128)(2,1)} %get-tuple-element.305), channel_id=1, source_target_pairs={{0,16},{8,24},{16,0},{24,8},{1,17},{9,25},{17,1},{25,9},{2,18},{10... | collective-permute-start | bytes 3145736 | tf_op jit(solution)/shard_map/ppermute | solution.py:428
  31.6 45.2 %collective-permute-start.5 = (bf16[256,2048]{1,0:T(8,128)(2,1)S(1)}, bf16[256,2048]{1,0:T(8,128)(2,1)}, u32[]{:S(2)}, u32[]{:S(2)}) collective-permute-start(bf16[256,2048]{1,0:T(8,128)(2,1)S(1)} %copy-done.18), channel_id=1, source_target_pairs={{0,8},{8,0},{16,24},{24,16},{1,9},{9,1},{17,25},{25,17},{2,10},{10... | collective-permute-start | bytes 3145736 | tf_op jit(solution)/shard_map/ppermute | solution.py:428
  32.2 47.9 %collective-permute-start.6 = (bf16[256,2048]{1,0:T(8,128)(2,1)S(1)}, bf16[256,2048]{1,0:T(8,128)(2,1)}, u32[]{:S(2)}, u32[]{:S(2)}) collective-permute-start(bf16[256,2048]{1,0:T(8,128)(2,1)S(1)} %copy-done.18), channel_id=1, source_target_pairs={{0,16},{8,24},{16,0},{24,8},{1,17},{9,25},{17,1},{25,9},{2,18},{10... | collective-permute-start | bytes 3145736 | tf_op jit(solution)/shard_map/ppermute | solution.py:428
  55.5 46.4 %collective-permute-start.3 = (bf16[128,2048]{1,0:T(8,128)(2,1)S(1)}, bf16[128,2048]{1,0:T(8,128)(2,1)S(1)}, u32[]{:S(2)}, u32[]{:S(2)}) collective-permute-start(bf16[128,2048]{1,0:T(8,128)(2,1)S(1)} %slice.368), channel_id=1, source_target_pairs={{0,16},{8,24},{16,0},{24,8},{1,17},{9,25},{17,1},{25,9},{2,18},{10... | collective-permute-start | bytes 1572872 | tf_op jit(solution)/shard_map/ppermute | solution.py:428
  58.7 44.0 %collective-permute-start.4 = (bf16[128,2048]{1,0:T(8,128)(2,1)S(1)}, bf16[128,2048]{1,0:T(8,128)(2,1)S(1)}, u32[]{:S(2)}, u32[]{:S(2)}) collective-permute-start(bf16[128,2048]{1,0:T(8,128)(2,1)S(1)} %slice.369), channel_id=1, source_target_pairs={{0,8},{8,0},{16,24},{24,16},{1,9},{9,1},{17,25},{25,17},{2,10},{10... | collective-permute-start | bytes 1572872 | tf_op jit(solution)/shard_map/ppermute | solution.py:428
  150.1 173.5 %all-gather.12.cloned.1.call-start = ((), (), s32[]{:S(2)}) async-start(), calls=%async_computation.15 | async-start | bytes 9437184 | tf_op jit(solution)/shard_map/all_gather | solution.py:497
  196.4 151.9 %all-gather.14.cloned.1.call-start = ((), (), s32[]{:S(2)}) async-start(), calls=%async_computation.16 | async-start | bytes 4718592 | tf_op jit(solution)/shard_map/all_gather | solution.py:497
  230.5 27.3 %collective-permute-start.11 = (bf16[256,2048]{1,0:T(8,128)(2,1)}, bf16[256,2048]{1,0:T(8,128)(2,1)}, u32[]{:S(2)}, u32[]{:S(2)}) collective-permute-start(bf16[256,2048]{1,0:T(8,128)(2,1)} %get-tuple-element.177), channel_id=1, source_target_pairs={{0,24},{8,16},{16,8},{24,0},{1,25},{9,17},{17,9},{25,1},{2,26},{10... | collective-permute-start | bytes 3145736 | tf_op jit(solution)/shard_map/ppermute | solution.py:428
  231.5 47.6 %collective-permute-start.12 = (bf16[256,2048]{1,0:T(8,128)(2,1)S(1)}, bf16[256,2048]{1,0:T(8,128)(2,1)}, u32[]{:S(2)}, u32[]{:S(2)}) collective-permute-start(bf16[256,2048]{1,0:T(8,128)(2,1)S(1)} %get-tuple-element.178), channel_id=1, source_target_pairs={{0,16},{8,24},{16,0},{24,8},{1,17},{9,25},{17,1},{25,9},{2,18},{10... | collective-permute-start | bytes 3145736 | tf_op jit(solution)/shard_map/ppermute | solution.py:428
  232.1 47.1 %collective-permute-start.13 = (bf16[256,2048]{1,0:T(8,128)(2,1)S(1)}, bf16[256,2048]{1,0:T(8,128)(2,1)}, u32[]{:S(2)}, u32[]{:S(2)}) collective-permute-start(bf16[256,2048]{1,0:T(8,128)(2,1)S(1)} %get-tuple-element.179), channel_id=1, source_target_pairs={{0,8},{8,0},{16,24},{24,16},{1,9},{9,1},{17,25},{25,17},{2,10},{10... | collective-permute-start | bytes 3145736 | tf_op jit(solution)/shard_map/ppermute | solution.py:428
  234.0 218.6 %reduce-scatter.6.cloned.1.call-start = ((), (), s32[]{:S(2)}) async-start(), calls=%async_computation.17 | async-start | bytes 4718592 | tf_op jit(solution)/shard_map/reduce_scatter | solution.py:500
  348.0 155.1 %reduce-scatter.8.cloned.1.call-start = ((), (), s32[]{:S(2)}) async-start(), calls=%async_computation.18 | async-start | bytes 9437184 | tf_op jit(solution)/shard_map/reduce_scatter | solution.py:500
  452.6 29.7 %collective-permute-start.26 = (bf16[256,1024]{1,0:T(8,128)(2,1)}, bf16[256,1024]{1,0:T(8,128)(2,1)S(1)}, u32[]{:S(2)}, u32[]{:S(2)}) collective-permute-start(bf16[256,1024]{1,0:T(8,128)(2,1)} %reduce-scatter.6.cloned.1.call-done.refs_0_), channel_id=1, source_target_pairs={{0,8},{8,0},{16,24},{24,16},{1,9},{9,1},{17,25},{25,17},{2,10},{10... | collective-permute-start | bytes 1572872 | tf_op jit(solution)/shard_map/ppermute | solution.py:428
  453.9 28.3 %collective-permute-start.27 = (bf16[256,1024]{1,0:T(8,128)(2,1)}, bf16[256,1024]{1,0:T(8,128)(2,1)S(1)}, u32[]{:S(2)}, u32[]{:S(2)}) collective-permute-start(bf16[256,1024]{1,0:T(8,128)(2,1)} %reduce-scatter.6.cloned.1.call-done.refs_0_), channel_id=1, source_target_pairs={{0,16},{8,24},{16,0},{24,8},{1,17},{9,25},{17,1},{25,9},{2,18},{10... | collective-permute-start | bytes 1572872 | tf_op jit(solution)/shard_map/ppermute | solution.py:428
  469.0 30.8 %collective-permute-start.28 = (bf16[1024,256]{1,0:T(8,128)(2,1)S(1)}, bf16[1024,256]{1,0:T(8,128)(2,1)S(1)}, u32[]{:S(2)}, u32[]{:S(2)}) collective-permute-start(bf16[1024,256]{1,0:T(8,128)(2,1)S(1)} %slice_select_fusion), channel_id=1, source_target_pairs={{0,16},{8,24},{16,0},{24,8},{1,17},{9,25},{17,1},{25,9},{2,18},{10... | collective-permute-start | bytes 1572872 | tf_op jit(solution)/shard_map/ppermute | solution.py:428
  487.7 86.2 %reduce-scatter.12.cloned.1.call-start = ((), (), s32[]{:S(2)}) async-start(), calls=%async_computation.20 | async-start | bytes 4718592 | tf_op jit(solution)/shard_map/reduce_scatter | solution.py:500
  503.9 46.2 %collective-permute-start.31 = (bf16[256,2048]{1,0:T(8,128)(2,1)}, bf16[256,2048]{1,0:T(8,128)(2,1)S(1)}, u32[]{:S(2)}, u32[]{:S(2)}) collective-permute-start(bf16[256,2048]{1,0:T(8,128)(2,1)} %reduce-scatter.8.cloned.1.call-done.refs_0_), channel_id=1, source_target_pairs={{0,8},{8,0},{16,24},{24,16},{1,9},{9,1},{17,25},{25,17},{2,10},{10... | collective-permute-start | bytes 3145736 | tf_op jit(solution)/shard_map/ppermute | solution.py:428
  504.8 45.3 %collective-permute-start.32 = (bf16[256,2048]{1,0:T(8,128)(2,1)}, bf16[256,2048]{1,0:T(8,128)(2,1)S(1)}, u32[]{:S(2)}, u32[]{:S(2)}) collective-permute-start(bf16[256,2048]{1,0:T(8,128)(2,1)} %reduce-scatter.8.cloned.1.call-done.refs_0_), channel_id=1, source_target_pairs={{0,16},{8,24},{16,0},{24,8},{1,17},{9,25},{17,1},{25,9},{2,18},{10... | collective-permute-start | bytes 3145736 | tf_op jit(solution)/shard_map/ppermute | solution.py:428
  508.5 28.3 %all-to-all-start.5 = ((bf16[8,64,512]{2,1,0:T(8,128)(2,1)}), bf16[8,64,512]{2,1,0:T(8,128)(2,1)}, u32[]{:S(2)}, u32[]{:S(2)}) async-start(bf16[8,64,512]{2,1,0:T(8,128)(2,1)} %pad_maximum_fusion.14), calls=%async_computation.7 | async-start | bytes 1048576 | tf_op jit(solution)/shard_map/all_to_all | solution.py:587
  512.6 164.8 %reduce-scatter.10.cloned.1.call-start = ((), (), s32[]{:S(2)}) async-start(), calls=%async_computation.19 | async-start | bytes 9437184 | tf_op jit(solution)/shard_map/reduce_scatter | solution.py:500
  564.2 154.3 %reduce-scatter.14.cloned.1.call-start = ((), (), s32[]{:S(2)}) async-start(), calls=%async_computation.21 | async-start | bytes 4718592 | tf_op jit(solution)/shard_map/reduce_scatter | solution.py:500
  568.2 37.1 %collective-permute-start.35 = (bf16[256,2048]{1,0:T(8,128)(2,1)}, bf16[256,2048]{1,0:T(8,128)(2,1)}, u32[]{:S(2)}, u32[]{:S(2)}) collective-permute-start(bf16[256,2048]{1,0:T(8,128)(2,1)} %pad_maximum_fusion.8), channel_id=1, source_target_pairs={{0,8},{8,0},{16,24},{24,16},{1,9},{9,1},{17,25},{25,17},{2,10},{10... | collective-permute-start | bytes 3145736 | tf_op jit(solution)/shard_map/ppermute | solution.py:428
  569.3 36.0 %collective-permute-start.36 = (bf16[256,2048]{1,0:T(8,128)(2,1)}, bf16[256,2048]{1,0:T(8,128)(2,1)}, u32[]{:S(2)}, u32[]{:S(2)}) collective-permute-start(bf16[256,2048]{1,0:T(8,128)(2,1)} %pad_maximum_fusion.9), channel_id=1, source_target_pairs={{0,16},{8,24},{16,0},{24,8},{1,17},{9,25},{17,1},{25,9},{2,18},{10... | collective-permute-start | bytes 3145736 | tf_op jit(solution)/shard_map/ppermute | solution.py:428
  571.6 33.6 %collective-permute-start.33 = (bf16[128,2048]{1,0:T(8,128)(2,1)}, bf16[128,2048]{1,0:T(8,128)(2,1)S(1)}, u32[]{:S(2)}, u32[]{:S(2)}) collective-permute-start(bf16[128,2048]{1,0:T(8,128)(2,1)} %slice.394), channel_id=1, source_target_pairs={{0,16},{8,24},{16,0},{24,8},{1,17},{9,25},{17,1},{25,9},{2,18},{10... | collective-permute-start | bytes 1572872 | tf_op jit(solution)/shard_map/ppermute | solution.py:428
  573.0 32.3 %collective-permute-start.34 = (bf16[128,2048]{1,0:T(8,128)(2,1)}, bf16[128,2048]{1,0:T(8,128)(2,1)S(1)}, u32[]{:S(2)}, u32[]{:S(2)}) collective-permute-start(bf16[128,2048]{1,0:T(8,128)(2,1)} %slice.395), channel_id=1, source_target_pairs={{0,8},{8,0},{16,24},{24,16},{1,9},{9,1},{17,25},{25,17},{2,10},{10... | collective-permute-start | bytes 1572872 | tf_op jit(solution)/shard_map/ppermute | solution.py:428
  648.5 31.7 %collective-permute-start.49 = (bf16[128,2048]{1,0:T(8,128)(2,1)}, bf16[128,2048]{1,0:T(8,128)(2,1)}, u32[]{:S(2)}, u32[]{:S(2)}) collective-permute-start(bf16[128,2048]{1,0:T(8,128)(2,1)} %get-tuple-element.270), channel_id=1, source_target_pairs={{0,16},{8,24},{16,0},{24,8},{1,17},{9,25},{17,1},{25,9},{2,18},{10... | collective-permute-start | bytes 1572872 | tf_op jit(solution)/shard_map/ppermute | solution.py:428
  649.9 30.3 %collective-permute-start.50 = (bf16[128,2048]{1,0:T(8,128)(2,1)}, bf16[128,2048]{1,0:T(8,128)(2,1)}, u32[]{:S(2)}, u32[]{:S(2)}) collective-permute-start(bf16[128,2048]{1,0:T(8,128)(2,1)} %get-tuple-element.271), channel_id=1, source_target_pairs={{0,8},{8,0},{16,24},{24,16},{1,9},{9,1},{17,25},{25,17},{2,10},{10... | collective-permute-start | bytes 1572872 | tf_op jit(solution)/shard_map/ppermute | solution.py:428
  651.0 26.4 %collective-permute-start.45 = (bf16[128,1024]{1,0:T(8,128)(2,1)S(1)}, bf16[128,1024]{1,0:T(8,128)(2,1)S(1)}, u32[]{:S(2)}, u32[]{:S(2)}) collective-permute-start(bf16[128,1024]{1,0:T(8,128)(2,1)S(1)} %slice.400), channel_id=1, source_target_pairs={{0,16},{8,24},{16,0},{24,8},{1,17},{9,25},{17,1},{25,9},{2,18},{10... | collective-permute-start | bytes 786440 | tf_op jit(solution)/shard_map/ppermute | solution.py:428
  (96 other events, 1252.1 us)
Sparse Core Ops, SparseCore 0:
  17.1 84.6 all-gather.5
  103.4 51.1 all-gather.7
  156.2 58.3 all-gather.9
  216.1 80.7 all-gather.11
  298.3 46.3 all-gather.13
  348.1 47.1 reduce-scatter.5
  398.7 87.2 reduce-scatter.7
  503.2 56.2 reduce-scatter.11
  564.3 88.3 reduce-scatter.9
  654.9 50.4 reduce-scatter.13
where the time goes:
time: 776 us; the launch traced here: 765 us
  waiting for transfers between devices  275 us (35%)
  Pallas kernels  119 us (15%)
  matrix products  102 us (13%)
  starting transfers between devices  96 us (12%)
  local copies, waits for them, and re-layouts  81 us (10%)
  other arithmetic  66.9 us (9%)
  between operations  24.7 us (3%)
    ppermute x55, waiting for transfers between devices, swap(): return lax.ppermute(v, 'seq', [(i, i ^ d) for i in range(group)])  219 us
    pallas_call x8, Pallas kernels, head_call(): return list(call(*arrays))  94.1 us
    ppermute x55, starting transfers between devices, swap(): return lax.ppermute(v, 'seq', [(i, i ^ d) for i in range(group)])  64.6 us
    dot_general x5, matrix products, dot_tn(): lax.dot_general(left, right, (((0,), (0,)), ((), ())), preferred_element_...  52.3 us
    all_to_all x3, waiting for transfers between devices, exchange_states(): got = lax.all_to_all(cut, 'shard', split_axis=0, concat_axis=0, tiled=True)  29 us
    dot_general x3, matrix products, dot_nt(): lax.dot_general(left, right, (((1,), (1,)), ((), ())), preferred_element_...  25.9 us
    unnamed x101, local copies, waits for them, and re-layouts  25.6 us
    pallas_call x4, Pallas kernels, place_blocks(): pl.pallas_call(functools.partial(place_kernel, index), grid_spec=pltpu.Pr...  25.3 us
  transfers between devices with their start and end apart: 82, of which 41 were waited for; matrix products, arithmetic and copies ran while one was open for 31% of the time, Pallas kernels for 14%

commit v1 on v0

--- a/solution.py
+++ b/solution.py
@@ -438,7 +438,7 @@
             h = v.shape[0] // 2
             r1 = swap(v, 1)
             r2 = swap(v, 2)
-            if beside is not None:
+            if beside:
                 r1, r2, beside[:] = tie(r1, r2, list(beside))
             return [(v,), (r1,), (r2,), (swap(r1[:h], 2), swap(r2[h:], 1))]
         return [(v,)] + [(swap(v, d),) for d in range(1, group)]
@@ -773,8 +773,6 @@
         d_swapped = swap(jnp.where(low, d_gates[0][:, DK:], d_gates[1][:, DK:]), 2)
     else:
         d_swapped = totals[0]
-    if group == 4:
-        totals[0], parts_ffn_out[:3] = tie_parts(totals[0], parts_ffn_out[:3])
     hidden, totals[0] = tie(hidden, totals[0])
     g_mixer_out = dot_tn(d_attn, hidden, BF16)
     inners = head_call(
@@ -877,6 +875,10 @@
     else:
         late = send_blocks(near_rows(ffn_terms))
     by_units[0], parts_ffn_in[:3] = tie_parts(by_units[0], parts_ffn_in[:3])
+    if group == 4:
+        ffn_own, ra, rb = late
+        by_units[0], ra, rb = tie(by_units[0], ra, rb)
+        late = ffn_own, ra, rb
     g_units = [dot_tn(by_units[0], normed, BF16)]
     by_units[-1], g_units[0] = tie(by_units[-1], g_units[0])
     by_units[-1], scattered["mixer_out"] = tie(by_units[-1], scattered["mixer_out"])
@@ -894,7 +896,6 @@
     d_normed, parts_ffn_in = tie_parts(d_normed, parts_ffn_in)
     if group == 4:
         ffn_own, ra, rb = late
-        d_normed, ra, rb = tie(d_normed, ra, rb)
         first = first_step(seq_rows(d_normed))
         output = (resid + second_step(ffn_own, ra, rb)).astype(BF16)
     else:
@@ -924,20 +925,14 @@
     ignored8, norm1_back = jax.vjp(rms_scale, xf, gain_attn)
     d_x_part, d_gain_attn = norm1_back(d_normed)
     input_grad = (d_resid + d_x_part).astype(BF16)
-    gains = jnp.concatenate([d_gain_attn, d_gain_ffn])[None]
-    step = 1
-    while step < group:
-        gains = gains + swap(gains, step)
-        step *= 2
-    g_slots[0], gains = tie(g_slots[0], gains)
     gains = lax.all_to_all(
-        jnp.broadcast_to(gains, (segments, 2 * width)),
+        jnp.broadcast_to(jnp.concatenate([d_gain_attn, d_gain_ffn])[None], (segments, 2 * width)),
         "shard",
         split_axis=0,
         concat_axis=0,
         tiled=True,
     )
-    gains = jnp.sum(gains, axis=0)
+    gains = jnp.sum(gains, axis=0, keepdims=True)
     parts = []
     for h in range(local_heads):
         last = h == local_heads - 1
@@ -957,10 +952,22 @@
             beside = [g_mixer_out, output, gains]
         if last and h > 0:
             g_slots[h], gains, g_mixer_out = tie(g_slots[h], gains, g_mixer_out)
+            beside = []
             g_slots[h], parts = tie_parts(g_slots[h], parts)
         here = spread(g_slots[h], beside)
         if group == 4 and h == 0:
             g_mixer_out, output, gains = beside
+        if last:
+            if beside is not None and group == 4:
+                here[1], gains = tie(here[1], gains)
+                gains = gains + swap(gains, 1)
+                here[3], gains = tie(here[3], gains)
+                gains = gains + swap(gains, 2)
+            else:
+                step = 1
+                while step < group:
+                    gains = gains + swap(gains, step)
+                    step *= 2
         if balanced and last:
             there = [tuple(cross(piece, 1) for piece in part) for part in here]
             parts += [a + b for a, b in zip(here, there)] + [b + a for a, b in zip(here, there)]
@@ -970,7 +977,7 @@
             parts += here + [
                 (cross(pick(stack, s ^ lend_here[n]), 1),) for n in range(lend_here.shape[0])
             ]
-    gain_attn_grad, gain_ffn_grad = gains[:width], gains[width:]
+    gain_attn_grad, gain_ffn_grad = gains[0, :width], gains[0, width:]
     found = back[j]
     if balanced:
         spare = lend.shape[-1]

time: 776 us -> 781 us (level)
    unnamed x101 -> x95, local copies, waits for them, and re-layouts: 25.6 us -> 26 us
  transfers between devices with their start and end apart: 82 -> 82, of which waited for: 41 -> 42; matrix products, arithmetic and copies ran while one was open for 31% -> 30% of each run, Pallas kernels for 14% -> 14%
where the time goes in v1:
time: 781 us; the launch traced here: 770 us
  waiting for transfers between devices  282 us (36%)
  Pallas kernels  119 us (15%)
  matrix products  103 us (13%)
  starting transfers between devices  94.3 us (12%)
  local copies, waits for them, and re-layouts  81.7 us (10%)
  other arithmetic  65.2 us (8%)
  between operations  24.6 us (3%)
    ppermute x55, waiting for transfers between devices, swap(): return lax.ppermute(v, 'seq', [(i, i ^ d) for i in range(group)])  224 us
    pallas_call x8, Pallas kernels, head_call(): return list(call(*arrays))  94.1 us
    ppermute x55, starting transfers between devices, swap(): return lax.ppermute(v, 'seq', [(i, i ^ d) for i in range(group)])  60 us
    dot_general x5, matrix products, dot_tn(): lax.dot_general(left, right, (((0,), (0,)), ((), ())), preferred_element_...  52.2 us
    dot_general x3, matrix products, dot_nt(): lax.dot_general(left, right, (((1,), (1,)), ((), ())), preferred_element_...  26.6 us
    unnamed x95, local copies, waits for them, and re-layouts  26 us
    all_to_all x3, waiting for transfers between devices, exchange_states(): got = lax.all_to_all(cut, 'shard', split_axis=0, concat_axis=0, tiled=True)  25.9 us
    pallas_call x4, Pallas kernels, place_blocks(): pl.pallas_call(functools.partial(place_kernel, index), grid_spec=pltpu.Pr...  25.3 us
  transfers between devices with their start and end apart: 82, of which 42 were waited for; matrix products, arithmetic and copies ran while one was open for 30% of the time, Pallas kernels for 14%

profile of v1, /device:TPU:0, one launch (start us, length us, event | category | flops | bytes accessed | tf_op | source)
XLA Modules:
  0.0 770.3 jit_solution(8589820252401725680)
XLA Ops:
  43.2 11.2 %collective-permute-done.1 = bf16[256,2048]{1,0:T(8,128)(2,1)} collective-permute-done((bf16[256,2048]{1,0:T(8,128)(2,1)}, bf16[256,2048]{1,0:T(8,128)(2,1)}, u32[]{:S(2)}, u32[]{:S(2)}) %collective-permute-start.1) | collective-permute-done | bytes 1048608 | tf_op jit(solution)/shard_map/ppermute | solution.py:428
  60.3 16.6 %collective-permute-done.5 = bf16[256,2048]{1,0:T(8,128)(2,1)} collective-permute-done((bf16[256,2048]{1,0:T(8,128)(2,1)S(1)}, bf16[256,2048]{1,0:T(8,128)(2,1)}, u32[]{:S(2)}, u32[]{:S(2)}) %collective-permute-start.5) | collective-permute-done | bytes 1048608 | tf_op jit(solution)/shard_map/ppermute | solution.py:428
  92.1 8.1 %collective-permute-done.7 = bf16[128,2048]{1,0:T(8,128)(2,1)S(1)} collective-permute-done((bf16[128,2048]{1,0:T(8,128)(2,1)S(1)}, bf16[128,2048]{1,0:T(8,128)(2,1)S(1)}, u32[]{:S(2)}, u32[]{:S(2)}) %collective-permute-start.7) | collective-permute-done | bytes 524320 | tf_op jit(solution)/shard_map/ppermute | solution.py:428
  107.0 16.3 %shard_map.197 = (bf16[1024,256]{1,0:T(8,128)(2,1)}, bf16[1024,256]{1,0:T(8,128)(2,1)}, bf16[1024,512]{1,0:T(8,128)(2,1)}, bf16[256,512]{1,0:T(8,128)(2,1)}, bf1...) custom-call(f32[2]{0:T(128)} %get-tuple-element.374.params, bf16[1024,2048]{1,0:T(8,128)(2,1)} %constant_dynamic-update-slice_fusion.17.x, ...), custom_call_target="tpu_custom_call" | custom-call | flops 8589934592 | bytes 18089992 | tf_op jit(solution)/shard_map/pallas_call | solution.py:363
  130.7 14.6 %all-to-all-done = bf16[8,32,512]{2,1,0:T(8,128)(2,1)S(1)} async-done(((bf16[8,32,512]{2,1,0:T(8,128)(2,1)}), bf16[8,32,512]{2,1,0:T(8,128)(2,1)S(1)}, u32[]{:S(2)}, u32[]{:S(2)}) %all-to-all-start) | async-done | bytes 262176 | tf_op jit(solution)/shard_map/all_to_all | solution.py:573
  159.7 10.7 %shard_map.198 = (bf16[1024,256]{1,0:T(8,128)(2,1)}, bf16[1024,256]{1,0:T(8,128)(2,1)}, bf16[1024,512]{1,0:T(8,128)(2,1)}, bf16[256,512]{1,0:T(8,128)(2,1)}, bf16[1024,256]{1,0:T(8,128)(2,1)}) custom-call(f32[2]{0:T(128)} %get-tuple-element.375.params, bf16[1024,2048]{1,0:T(8,128)(2,1)} %constant_dynamic-update-slice_fusion.17.x, ...), custom_call_target="tpu_custom_call" | custom-call | flops 4294967296 | bytes 12847112 | tf_op jit(solution)/shard_map/pallas_call | solution.py:363
  180.1 11.3 %all-to-all-done.2 = bf16[8,32,512]{2,1,0:T(8,128)(2,1)S(1)} async-done(((bf16[8,32,512]{2,1,0:T(8,128)(2,1)}), bf16[8,32,512]{2,1,0:T(8,128)(2,1)S(1)}, u32[]{:S(2)}, u32[]{:S(2)}) %all-to-all-start.2) | async-done | bytes 262176 | tf_op jit(solution)/shard_map/all_to_all | solution.py:573
  220.9 7.9 %convolution_convert_fusion.7 = bf16[1024,2048]{1,0:T(8,128)(2,1)S(1)} fusion(bf16[1024,1024]{1,0:T(8,128)(2,1)} %constant_dynamic-update-slice_fusion.5, bf16[2048,1024]{1,0:T(8,128)(2,1)} %all-gather.10.cloned.1.call-done.w_out), kind=kOutput, calls=%fused_computation.30 | convolution fusion | flops 4297064448 | bytes 10485760 | tf_op jit(solution)/shard_map/dot_general | solution.py:26
  234.7 23.2 %collective-permute-done.11 = bf16[256,2048]{1,0:T(8,128)(2,1)} collective-permute-done((bf16[256,2048]{1,0:T(8,128)(2,1)}, bf16[256,2048]{1,0:T(8,128)(2,1)}, u32[]{:S(2)}, u32[]{:S(2)}) %collective-permute-start.11) | collective-permute-done | bytes 1048608 | tf_op jit(solution)/shard_map/ppermute | solution.py:428
  257.9 21.2 %collective-permute-done.12 = bf16[256,2048]{1,0:T(8,128)(2,1)} collective-permute-done((bf16[256,2048]{1,0:T(8,128)(2,1)S(1)}, bf16[256,2048]{1,0:T(8,128)(2,1)}, u32[]{:S(2)}, u32[]{:S(2)}) %collective-permute-start.12) | collective-permute-done | bytes 1048608 | tf_op jit(solution)/shard_map/ppermute | solution.py:428
  285.7 23.0 %collective-permute-done.14 = bf16[256,2048]{1,0:T(8,128)(2,1)S(1)} collective-permute-done((bf16[256,2048]{1,0:T(8,128)(2,1)S(1)}, bf16[256,2048]{1,0:T(8,128)(2,1)S(1)}, u32[]{:S(2)}, u32[]{:S(2)}) %collective-permute-start.14) | collective-permute-done | bytes 1048608 | tf_op jit(solution)/shard_map/ppermute | solution.py:428
  313.1 8.6 %collective-permute-done.16 = bf16[128,2048]{1,0:T(8,128)(2,1)S(1)} collective-permute-done((bf16[128,2048]{1,0:T(8,128)(2,1)S(1)}, bf16[128,2048]{1,0:T(8,128)(2,1)S(1)}, u32[]{:S(2)}, u32[]{:S(2)}) %collective-permute-start.16) | collective-permute-done | bytes 524320 | tf_op jit(solution)/shard_map/ppermute | solution.py:428
  323.3 12.6 %fusion.48 = f32[1024,2048]{1,0:T(8,128)S(1)} fusion(bf16[1024,2048]{1,0:T(8,128)(2,1)} %constant_dynamic-update-slice_fusion.7, bf16[2048,2048]{1,0:T(8,128)(2,1)} %all-gather.12.cloned.1.call-done), kind=kOutput, calls=%fused_computation.194 | convolution fusion | flops 8589934592 | bytes 20971520 | tf_op jit(solution)/shard_map/dot_general | solution.py:26
  348.0 12.5 %fusion.6 = (bf16[1024,1024]{1,0:T(8,128)(2,1)S(1)}, bf16[1024,1024]{1,0:T(8,128)(2,1)S(1)}) fusion(f32[1024,2048]{1,0:T(8,128)} %copy-done.10, bf16[1024,2048]{1,0:T(8,128)(2,1)} %constant_dynamic-update-slice_fusion, bf16[2048,1024]{0,1:T(8,128)(2,1)} %all-gather.14.cloned.1.call-done), kind=kOutput, calls=%fused_computation.10 | convolution fusion | flops 4320133120 | bytes 20971520 | tf_op jit(solution)/shard_map/dot_general | solution.py:32
  360.6 11.4 %convolution_convert_fusion.2 = bf16[1024,2048]{1,0:T(8,128)(2,1)S(1)} fusion(bf16[2048,2048]{1,0:T(8,128)(2,1)} %all-gather.12.cloned.1.call-done, bf16[1024,1024]{1,0:T(8,128)(2,1)S(1)} %get-tuple-element.307, bf16[1024,1024]{1,0:T(8,128)(2,1)S(1)} %get-tuple-element.306), kind=kOutput, calls=%fused_computation.25 | convolution fusion | flops 8600420352 | bytes 16777216 | tf_op jit(solution)/shard_map/dot_general | solution.py:32
  376.6 14.2 %convolution_convert_fusion.1 = bf16[2048,2048]{1,0:T(8,128)(2,1)} fusion(bf16[1024,2048]{1,0:T(8,128)(2,1)} %constant_dynamic-update-slice_fusion.7, bf16[1024,1024]{1,0:T(8,128)(2,1)S(1)} %get-tuple-element.307, bf16[1024,1024]{1,0:T(8,128)(2,1)S(1)} %get-tuple-element.306), kind=kOutput, calls=%fused_computation.1 | convolution fusion | flops 8602517504 | bytes 16777216 | tf_op jit(solution)/shard_map/dot_general | solution.py:38
  403.2 8.7 %collective-permute-done.20 = bf16[128,2048]{1,0:T(8,128)(2,1)S(1)} collective-permute-done((bf16[128,2048]{1,0:T(8,128)(2,1)S(1)}, bf16[128,2048]{1,0:T(8,128)(2,1)S(1)}, u32[]{:S(2)}, u32[]{:S(2)}) %collective-permute-start.20) | collective-permute-done | bytes 524320 | tf_op jit(solution)/shard_map/ppermute | solution.py:428
  418.5 18.9 %collective-permute-done.22 = bf16[256,2048]{1,0:T(8,128)(2,1)S(1)} collective-permute-done((bf16[256,2048]{1,0:T(8,128)(2,1)S(1)}, bf16[256,2048]{1,0:T(8,128)(2,1)S(1)}, u32[]{:S(2)}, u32[]{:S(2)}) %collective-permute-start.22) | collective-permute-done | bytes 1048608 | tf_op jit(solution)/shard_map/ppermute | solution.py:428
  454.8 13.3 %shard_map.201 = (bf16[1024,512]{1,0:T(8,128)(2,1)}, bf16[1024,512]{1,0:T(8,128)(2,1)}, bf16[256,512]{1,0:T(8,128)(2,1)}, bf16[1024,512]{1,0:T(8,128)(2,1)}, bf1...) custom-call(f32[4]{0:T(128)} %pad_maximum_fusion.16.params, ...), custom_call_target="tpu_custom_call" | custom-call | flops 4831838208 | bytes 25702416 | tf_op jit(solution)/shard_map/pallas_call | solution.py:363
  477.6 9.4 %convolution_convert_fusion.5 = bf16[2048,1024]{1,0:T(8,128)(2,1)} fusion(bf16[1024,2048]{1,0:T(8,128)(2,1)} %constant_dynamic-update-slice_fusion.12.d_attn, bf16[1024,1024]{1,0:T(8,128)(2,1)} %constant_dynamic-update-slice_fusion.5), kind=kOutput, calls=%fused_computation.28 | convolution fusion | flops 4297064448 | bytes 10485760 | tf_op jit(solution)/shard_map/dot_general | solution.py:38
  489.4 11.5 %shard_map.202 = (bf16[1024,256]{1,0:T(8,128)(2,1)}, f32[1024,256]{1,0:T(8,128)}, f32[1024,512]{1,0:T(8,128)}, bf16[1024,256]{1,0:T(8,128)(2,1)}, f32[1024,256]{1,0:T(8,128)}, /*index=5*/f32[1024,512]{1,0:T(8,128)}) custom-call(f32[4]{0:T(128)} %pad_maximum_fusion.16.params, f32[1024,128]{1,0:T(8,128)} %get-tuple-element.150.cosine, ...), custom_call_target="tpu_custom_call" | custom-call | flops 4831838208 | bytes 17309712 | tf_op jit(solution)/shard_map/pallas_call | solution.py:363
  527.9 8.9 %all-to-all-done.5 = bf16[8,64,512]{2,1,0:T(8,128)(2,1)} async-done(((bf16[8,64,512]{2,1,0:T(8,128)(2,1)}), bf16[8,64,512]{2,1,0:T(8,128)(2,1)}, u32[]{:S(2)}, u32[]{:S(2)}) %all-to-all-start.5) | async-done | bytes 524320 | tf_op jit(solution)/shard_map/all_to_all | solution.py:587
  542.6 11.3 %shard_map.204 = (bf16[1024,2048]{1,0:T(8,128)(2,1)}, bf16[1024,1024]{1,0:T(8,128)(2,1)}) custom-call(f32[4]{0:T(128)} %pad_maximum_fusion.16.params, f32[1024,128]{1,0:T(8,128)} %get-tuple-element.150.cosine, f32[1024,128]{1,0:T(8,128)} %get-tuple-element.151.sine, bf16[1024,256]{1,0:T(8,128)(2,1)} %get-tuple-element.156.q.refs_6_.refs_0_, ...), custom_call_target="tpu_custom_call" | custom-call | flops 134217728 | bytes 28844048 | tf_op jit(solution)/shard_map/pallas_call | solution.py:363
  554.0 11.3 %collective-permute-done.33 = bf16[256,2048]{1,0:T(8,128)(2,1)} collective-permute-done((bf16[256,2048]{1,0:T(8,128)(2,1)S(1)}, bf16[256,2048]{1,0:T(8,128)(2,1)}, u32[]{:S(2)}, u32[]{:S(2)}) %collective-permute-start.33) | collective-permute-done | bytes 1048608 | tf_op jit(solution)/shard_map/ppermute | solution.py:428
  565.9 14.0 %convolution_convert_fusion = bf16[2048,2048]{1,0:T(8,128)(2,1)} fusion(bf16[1024,2048]{1,0:T(8,128)(2,1)} %get-tuple-element.233.refs_0_, bf16[1024,2048]{1,0:T(8,128)(2,1)} %constant_dynamic-update-slice_fusion.17.x), kind=kOutput, calls=%fused_computation | convolution fusion | flops 8594128896 | bytes 16777216 | tf_op jit(solution)/shard_map/dot_general | solution.py:38
  583.6 18.9 %shard_map.205 = bf16[1024,2048]{1,0:T(8,128)(2,1)} custom-call(bf16[1024,2048]{1,0:T(8,128)(2,1)} %get-tuple-element.233.refs_0_, bf16[1024,1024]{1,0:T(8,128)(2,1)} %get-tuple-element.244.refs_1_, bf16[2048,2048]{1,0:T(8,128)(2,1)} %all-gather.6.cloned.1.call-done.w.refs_2_, bf16[1024,2048]{1,0:T(8,128)(2,1)} %all-gather.8.cloned.1.call-done.w.refs_3_), custom_call_target="tpu_custom_call" | custom-call | flops 2097152 | bytes 23068672 | tf_op jit(solution)/shard_map/pallas_call | solution.py:363
  614.6 8.3 %convolution_convert_fusion.3 = bf16[1024,2048]{1,0:T(8,128)(2,1)} fusion(bf16[1024,1024]{1,0:T(8,128)(2,1)S(1)} %copy-done.26, bf16[1024,2048]{1,0:T(8,128)(2,1)} %constant_dynamic-update-slice_fusion.17.x), kind=kOutput, calls=%fused_computation.26 | convolution fusion | flops 4297064448 | bytes 10485760 | tf_op jit(solution)/shard_map/dot_general | solution.py:38
  622.9 7.0 collective-permute-done.37
  651.8 9.9 %collective-permute-done.39 = bf16[128,2048]{1,0:T(8,128)(2,1)S(1)} collective-permute-done((bf16[128,2048]{1,0:T(8,128)(2,1)S(1)}, bf16[128,2048]{1,0:T(8,128)(2,1)S(1)}, u32[]{:S(2)}, u32[]{:S(2)}) %collective-permute-start.39) | collective-permute-done | bytes 524320 | tf_op jit(solution)/shard_map/ppermute | solution.py:428
  667.6 7.5 collective-permute-done.43.refs_3_
  727.7 11.6 %collective-permute-done.54.refs_10_ = bf16[128,2048]{1,0:T(8,128)(2,1)S(1)} collective-permute-done((bf16[128,2048]{1,0:T(8,128)(2,1)}, bf16[128,2048]{1,0:T(8,128)(2,1)S(1)}, u32[]{:S(2)}, u32[]{:S(2)}) %collective-permute-start.54) | collective-permute-done | bytes 524320 | tf_op jit(solution)/shard_map/ppermute | solution.py:428
  754.6 8.6 %shard_map.208 = f32[1536,2048]{1,0:T(8,128)} custom-call(s32[6]{0:T(128)S(1)} %iota.50.target, s32[6]{0:T(128)S(1)} %bitcast_select_fusion.3.source, bf16[256,2048]{1,0:T(8,128)(2,1)} %reduce-scatter.10.cloned.1.call-done.refs_0_, bf16[256,2048]{1,0:T(8,128)(2,1)} %copy-done.14, bf16[256,2048]{1,0:T(8,128)(2,1)} %collective-permute-done.46.refs_2_, ...), custom_call_target="tpu_custom_call" | custom-call | tf_op jit(solution)/shard_map/pallas_call | solution.py:387
  (388 shorter events, 343.1 us)
Async XLA Ops:
  7.2 96.4 %all-gather.6.cloned.1.call-start = ((), (), s32[]{:S(2)}) async-start(), calls=%async_computation.12 | async-start | bytes 9437184 | tf_op jit(solution)/shard_map/all_gather | solution.py:497
  16.9 139.6 %all-gather.8.cloned.1.call-start = ((), (), s32[]{:S(2)}) async-start(), calls=%async_computation.13 | async-start | bytes 4718592 | tf_op jit(solution)/shard_map/all_gather | solution.py:497
  22.7 198.2 %all-gather.10.cloned.1.call-start = ((), (), s32[]{:S(2)}) async-start(), calls=%async_computation.14 | async-start | bytes 4718592 | tf_op jit(solution)/shard_map/all_gather | solution.py:497
  27.3 27.1 %collective-permute-start.1 = (bf16[256,2048]{1,0:T(8,128)(2,1)}, bf16[256,2048]{1,0:T(8,128)(2,1)}, u32[]{:S(2)}, u32[]{:S(2)}) collective-permute-start(bf16[256,2048]{1,0:T(8,128)(2,1)} %get-tuple-element.303), channel_id=1, source_target_pairs={{0,8},{8,0},{16,24},{24,16},{1,9},{9,1},{17,25},{25,17},{2,10},{10... | collective-permute-start | bytes 3145736 | tf_op jit(solution)/shard_map/ppermute | solution.py:428
  30.1 27.5 %collective-permute-start.2 = (bf16[256,2048]{1,0:T(8,128)(2,1)}, bf16[256,2048]{1,0:T(8,128)(2,1)}, u32[]{:S(2)}, u32[]{:S(2)}) collective-permute-start(bf16[256,2048]{1,0:T(8,128)(2,1)} %get-tuple-element.303), channel_id=1, source_target_pairs={{0,16},{8,24},{16,0},{24,8},{1,17},{9,25},{17,1},{25,9},{2,18},{10... | collective-permute-start | bytes 3145736 | tf_op jit(solution)/shard_map/ppermute | solution.py:428
  31.7 45.2 %collective-permute-start.5 = (bf16[256,2048]{1,0:T(8,128)(2,1)S(1)}, bf16[256,2048]{1,0:T(8,128)(2,1)}, u32[]{:S(2)}, u32[]{:S(2)}) collective-permute-start(bf16[256,2048]{1,0:T(8,128)(2,1)S(1)} %copy-done.18), channel_id=1, source_target_pairs={{0,8},{8,0},{16,24},{24,16},{1,9},{9,1},{17,25},{25,17},{2,10},{10... | collective-permute-start | bytes 3145736 | tf_op jit(solution)/shard_map/ppermute | solution.py:428
  32.2 47.9 %collective-permute-start.6 = (bf16[256,2048]{1,0:T(8,128)(2,1)S(1)}, bf16[256,2048]{1,0:T(8,128)(2,1)}, u32[]{:S(2)}, u32[]{:S(2)}) collective-permute-start(bf16[256,2048]{1,0:T(8,128)(2,1)S(1)} %copy-done.18), channel_id=1, source_target_pairs={{0,16},{8,24},{16,0},{24,8},{1,17},{9,25},{17,1},{25,9},{2,18},{10... | collective-permute-start | bytes 3145736 | tf_op jit(solution)/shard_map/ppermute | solution.py:428
  55.5 46.4 %collective-permute-start.3 = (bf16[128,2048]{1,0:T(8,128)(2,1)S(1)}, bf16[128,2048]{1,0:T(8,128)(2,1)S(1)}, u32[]{:S(2)}, u32[]{:S(2)}) collective-permute-start(bf16[128,2048]{1,0:T(8,128)(2,1)S(1)} %slice.368), channel_id=1, source_target_pairs={{0,16},{8,24},{16,0},{24,8},{1,17},{9,25},{17,1},{25,9},{2,18},{10... | collective-permute-start | bytes 1572872 | tf_op jit(solution)/shard_map/ppermute | solution.py:428
  58.7 44.0 %collective-permute-start.4 = (bf16[128,2048]{1,0:T(8,128)(2,1)S(1)}, bf16[128,2048]{1,0:T(8,128)(2,1)S(1)}, u32[]{:S(2)}, u32[]{:S(2)}) collective-permute-start(bf16[128,2048]{1,0:T(8,128)(2,1)S(1)} %slice.369), channel_id=1, source_target_pairs={{0,8},{8,0},{16,24},{24,16},{1,9},{9,1},{17,25},{25,17},{2,10},{10... | collective-permute-start | bytes 1572872 | tf_op jit(solution)/shard_map/ppermute | solution.py:428
  150.1 173.3 %all-gather.12.cloned.1.call-start = ((), (), s32[]{:S(2)}) async-start(), calls=%async_computation.15 | async-start | bytes 9437184 | tf_op jit(solution)/shard_map/all_gather | solution.py:497
  196.2 151.8 %all-gather.14.cloned.1.call-start = ((), (), s32[]{:S(2)}) async-start(), calls=%async_computation.16 | async-start | bytes 4718592 | tf_op jit(solution)/shard_map/all_gather | solution.py:497
  230.6 27.3 %collective-permute-start.11 = (bf16[256,2048]{1,0:T(8,128)(2,1)}, bf16[256,2048]{1,0:T(8,128)(2,1)}, u32[]{:S(2)}, u32[]{:S(2)}) collective-permute-start(bf16[256,2048]{1,0:T(8,128)(2,1)} %get-tuple-element.176), channel_id=1, source_target_pairs={{0,24},{8,16},{16,8},{24,0},{1,25},{9,17},{17,9},{25,1},{2,26},{10... | collective-permute-start | bytes 3145736 | tf_op jit(solution)/shard_map/ppermute | solution.py:428
  231.6 47.5 %collective-permute-start.12 = (bf16[256,2048]{1,0:T(8,128)(2,1)S(1)}, bf16[256,2048]{1,0:T(8,128)(2,1)}, u32[]{:S(2)}, u32[]{:S(2)}) collective-permute-start(bf16[256,2048]{1,0:T(8,128)(2,1)S(1)} %get-tuple-element.177), channel_id=1, source_target_pairs={{0,16},{8,24},{16,0},{24,8},{1,17},{9,25},{17,1},{25,9},{2,18},{10... | collective-permute-start | bytes 3145736 | tf_op jit(solution)/shard_map/ppermute | solution.py:428
  232.2 47.1 %collective-permute-start.13 = (bf16[256,2048]{1,0:T(8,128)(2,1)S(1)}, bf16[256,2048]{1,0:T(8,128)(2,1)}, u32[]{:S(2)}, u32[]{:S(2)}) collective-permute-start(bf16[256,2048]{1,0:T(8,128)(2,1)S(1)} %get-tuple-element.178), channel_id=1, source_target_pairs={{0,8},{8,0},{16,24},{24,16},{1,9},{9,1},{17,25},{25,17},{2,10},{10... | collective-permute-start | bytes 3145736 | tf_op jit(solution)/shard_map/ppermute | solution.py:428
  234.1 218.1 %reduce-scatter.6.cloned.1.call-start = ((), (), s32[]{:S(2)}) async-start(), calls=%async_computation.17 | async-start | bytes 4718592 | tf_op jit(solution)/shard_map/reduce_scatter | solution.py:500
  283.8 24.9 %collective-permute-start.14 = (bf16[256,2048]{1,0:T(8,128)(2,1)S(1)}, bf16[256,2048]{1,0:T(8,128)(2,1)S(1)}, u32[]{:S(2)}, u32[]{:S(2)}) collective-permute-start(bf16[256,2048]{1,0:T(8,128)(2,1)S(1)} %get-tuple-element.299), channel_id=1, source_target_pairs={{0,8},{8,0},{16,24},{24,16},{1,9},{9,1},{17,25},{25,17},{2,10},{10... | collective-permute-start | bytes 3145736 | tf_op jit(solution)/shard_map/ppermute | solution.py:428
  284.3 24.9 %collective-permute-start.15 = (bf16[256,2048]{1,0:T(8,128)(2,1)S(1)}, bf16[256,2048]{1,0:T(8,128)(2,1)S(1)}, u32[]{:S(2)}, u32[]{:S(2)}) collective-permute-start(bf16[256,2048]{1,0:T(8,128)(2,1)S(1)} %get-tuple-element.299), channel_id=1, source_target_pairs={{0,16},{8,24},{16,0},{24,8},{1,17},{9,25},{17,1},{25,9},{2,18},{10... | collective-permute-start | bytes 3145736 | tf_op jit(solution)/shard_map/ppermute | solution.py:428
  347.8 153.9 %reduce-scatter.8.cloned.1.call-start = ((), (), s32[]{:S(2)}) async-start(), calls=%async_computation.18 | async-start | bytes 9437184 | tf_op jit(solution)/shard_map/reduce_scatter | solution.py:500
  452.2 34.8 %collective-permute-start.27 = (bf16[256,1024]{1,0:T(8,128)(2,1)}, bf16[256,1024]{1,0:T(8,128)(2,1)S(1)}, u32[]{:S(2)}, u32[]{:S(2)}) collective-permute-start(bf16[256,1024]{1,0:T(8,128)(2,1)} %reduce-scatter.6.cloned.1.call-done.refs_0_), channel_id=1, source_target_pairs={{0,8},{8,0},{16,24},{24,16},{1,9},{9,1},{17,25},{25,17},{2,10},{10... | collective-permute-start | bytes 1572872 | tf_op jit(solution)/shard_map/ppermute | solution.py:428
  452.5 35.2 %collective-permute-start.28 = (bf16[256,1024]{1,0:T(8,128)(2,1)}, bf16[256,1024]{1,0:T(8,128)(2,1)S(1)}, u32[]{:S(2)}, u32[]{:S(2)}) collective-permute-start(bf16[256,1024]{1,0:T(8,128)(2,1)} %reduce-scatter.6.cloned.1.call-done.refs_0_), channel_id=1, source_target_pairs={{0,16},{8,24},{16,0},{24,8},{1,17},{9,25},{17,1},{25,9},{2,18},{10... | collective-permute-start | bytes 1572872 | tf_op jit(solution)/shard_map/ppermute | solution.py:428
  469.3 31.6 %collective-permute-start.26 = (bf16[1024,256]{1,0:T(8,128)(2,1)S(1)}, bf16[1024,256]{1,0:T(8,128)(2,1)S(1)}, u32[]{:S(2)}, u32[]{:S(2)}) collective-permute-start(bf16[1024,256]{1,0:T(8,128)(2,1)S(1)} %slice_select_fusion), channel_id=1, source_target_pairs={{0,16},{8,24},{16,0},{24,8},{1,17},{9,25},{17,1},{25,9},{2,18},{10... | collective-permute-start | bytes 1572872 | tf_op jit(solution)/shard_map/ppermute | solution.py:428
  471.2 30.4 %all-to-all-start.4 = ((bf16[8,64,512]{2,1,0:T(8,128)(2,1)}), bf16[8,64,512]{2,1,0:T(8,128)(2,1)S(1)}, u32[]{:S(2)}, u32[]{:S(2)}) async-start(bf16[8,64,512]{2,1,0:T(8,128)(2,1)} %pad_maximum_fusion.13), calls=%async_computation.5 | async-start | bytes 1048576 | tf_op jit(solution)/shard_map/all_to_all | solution.py:573
  477.1 106.4 %reduce-scatter.12.cloned.1.call-start = ((), (), s32[]{:S(2)}) async-start(), calls=%async_computation.20 | async-start | bytes 4718592 | tf_op jit(solution)/shard_map/reduce_scatter | solution.py:500
  502.5 51.5 %collective-permute-start.31 = (bf16[256,2048]{1,0:T(8,128)(2,1)}, bf16[256,2048]{1,0:T(8,128)(2,1)S(1)}, u32[]{:S(2)}, u32[]{:S(2)}) collective-permute-start(bf16[256,2048]{1,0:T(8,128)(2,1)} %reduce-scatter.8.cloned.1.call-done.refs_0_), channel_id=1, source_target_pairs={{0,8},{8,0},{16,24},{24,16},{1,9},{9,1},{17,25},{25,17},{2,10},{10... | collective-permute-start | bytes 3145736 | tf_op jit(solution)/shard_map/ppermute | solution.py:428
  502.9 51.1 %collective-permute-start.32 = (bf16[256,2048]{1,0:T(8,128)(2,1)}, bf16[256,2048]{1,0:T(8,128)(2,1)S(1)}, u32[]{:S(2)}, u32[]{:S(2)}) collective-permute-start(bf16[256,2048]{1,0:T(8,128)(2,1)} %reduce-scatter.8.cloned.1.call-done.refs_0_), channel_id=1, source_target_pairs={{0,16},{8,24},{16,0},{24,8},{1,17},{9,25},{17,1},{25,9},{2,18},{10... | collective-permute-start | bytes 3145736 | tf_op jit(solution)/shard_map/ppermute | solution.py:428
  507.5 29.2 %all-to-all-start.5 = ((bf16[8,64,512]{2,1,0:T(8,128)(2,1)}), bf16[8,64,512]{2,1,0:T(8,128)(2,1)}, u32[]{:S(2)}, u32[]{:S(2)}) async-start(bf16[8,64,512]{2,1,0:T(8,128)(2,1)} %pad_maximum_fusion.14), calls=%async_computation.7 | async-start | bytes 1048576 | tf_op jit(solution)/shard_map/all_to_all | solution.py:587
  512.6 155.0 %reduce-scatter.10.cloned.1.call-start = ((), (), s32[]{:S(2)}) async-start(), calls=%async_computation.19 | async-start | bytes 9437184 | tf_op jit(solution)/shard_map/reduce_scatter | solution.py:500
  540.5 24.8 %collective-permute-start.33 = (bf16[256,2048]{1,0:T(8,128)(2,1)S(1)}, bf16[256,2048]{1,0:T(8,128)(2,1)}, u32[]{:S(2)}, u32[]{:S(2)}) collective-permute-start(bf16[256,2048]{1,0:T(8,128)(2,1)S(1)} %pad_maximum_fusion.8), channel_id=1, source_target_pairs={{0,8},{8,0},{16,24},{24,16},{1,9},{9,1},{17,25},{25,17},{2,10},{10... | collective-permute-start | bytes 3145736 | tf_op jit(solution)/shard_map/ppermute | solution.py:428
  579.9 140.3 %reduce-scatter.14.cloned.1.call-start = ((), (), s32[]{:S(2)}) async-start(), calls=%async_computation.21 | async-start | bytes 4718592 | tf_op jit(solution)/shard_map/reduce_scatter | solution.py:500
  644.9 31.6 %collective-permute-start.47 = (bf16[128,2048]{1,0:T(8,128)(2,1)}, bf16[128,2048]{1,0:T(8,128)(2,1)}, u32[]{:S(2)}, u32[]{:S(2)}) collective-permute-start(bf16[128,2048]{1,0:T(8,128)(2,1)} %get-tuple-element.264), channel_id=1, source_target_pairs={{0,16},{8,24},{16,0},{24,8},{1,17},{9,25},{17,1},{25,9},{2,18},{10... | collective-permute-start | bytes 1572872 | tf_op jit(solution)/shard_map/ppermute | solution.py:428
  649.8 26.7 %collective-permute-start.48 = (bf16[128,2048]{1,0:T(8,128)(2,1)}, bf16[128,2048]{1,0:T(8,128)(2,1)}, u32[]{:S(2)}, u32[]{:S(2)}) collective-permute-start(bf16[128,2048]{1,0:T(8,128)(2,1)} %get-tuple-element.265), channel_id=1, source_target_pairs={{0,8},{8,0},{16,24},{24,16},{1,9},{9,1},{17,25},{25,17},{2,10},{10... | collective-permute-start | bytes 1572872 | tf_op jit(solution)/shard_map/ppermute | solution.py:428
  650.5 24.6 %collective-permute-start.43 = (bf16[128,1024]{1,0:T(8,128)(2,1)S(1)}, bf16[128,1024]{1,0:T(8,128)(2,1)S(1)}, u32[]{:S(2)}, u32[]{:S(2)}) collective-permute-start(bf16[128,1024]{1,0:T(8,128)(2,1)S(1)} %slice.400), channel_id=1, source_target_pairs={{0,16},{8,24},{16,0},{24,8},{1,17},{9,25},{17,1},{25,9},{2,18},{10... | collective-permute-start | bytes 786440 | tf_op jit(solution)/shard_map/ppermute | solution.py:428
  (93 other events, 1244.4 us)
Sparse Core Ops, SparseCore 0:
  17.1 84.6 all-gather.5
  103.4 51.1 all-gather.7
  156.2 58.3 all-gather.9
  216.1 80.7 all-gather.11
  298.2 46.3 all-gather.13
  347.9 47.4 reduce-scatter.5
  398.7 89.4 reduce-scatter.7
  501.9 58.7 reduce-scatter.11
  580.1 87.4 reduce-scatter.9
  669.7 50.4 reduce-scatter.13
